TPU v7x, 512 devices: a whole 4x8x8 slice. The times are simulated.
512 devices in a mesh: face: 8 (over z_lo, core), tile: 64 (over x, z_hi, y).
Axes of the slice: x: 4, y: 8, z: 8 (z_hi: 2, z_lo: 4; z = z_hi * 4 + z_lo), core: 2. Of those that a mesh axis runs over, the one named last changes fastest.
Arguments:
- state_field: float32 [8, 64, 16, 16, 256], P('face', 'tile'), may hold values from -6 to 6
- out_grad: float32 [8, 64, 16, 16, 256], P('face', 'tile'), may hold values from -6 to 6
- depth_kernel: float32 [9, 256], P(None, 'tile'), may hold values from -2 to 2
- norm_gain: float32 [256], P('tile'), may hold values from 0.5 to 1.5
- up_weight: float32 [256, 1024], P('tile'), may hold values from -0.375 to 0.375
- down_weight: float32 [1024, 256], P('tile'), may hold values from -0.1875 to 0.1875
- seam_code: int32 [8, 64, 4], P('face', 'tile'), may hold values from 0 to 1, as said below
Outputs:
- new_field: float32 [8, 64, 16, 16, 256], P('face', 'tile')
- field_grad: float32 [8, 64, 16, 16, 256], P('face', 'tile')
- kernel_grad: float32 [9, 256], P(None, 'tile')
- gain_grad: float32 [256], P('tile')
- up_grad: float32 [256, 1024], P('tile')
- down_grad: float32 [1024, 256], P('tile')
Inputs may be any that keep to these rules, and one draw needn't show every extreme that they name: `seam_code`: 1 where the strip across a seam runs in reverse order; the same value on both sides of a seam; 0 on edges that do not lie on the face border.
All inputs are finite; a program needn't handle non-finite values.
Results may differ from a plain program's by a relative error of at most 0.00027.
Values sent between devices are 32-bit elements; how exact they have to be, the bound alone decides.
A program may use at most 64 MiB of HBM per device.

v0:
```python
import math

import jax
import jax.numpy as jnp
from jax import lax
from jax.sharding import PartitionSpec as P

EPSILON = 1e-06
PRECISE = lax.Precision.HIGHEST


def shifted(value, axis, steps):
    count = lax.axis_size(axis)
    initial, last = (max(0, -steps), min(count, count - steps))
    return lax.ppermute(value, axis, [(source, source + steps) for source in range(initial, last)])


def convnext_block(padded, kernel, gain_full, up_full, down_full):
    size_cells = padded.shape[-2] - 2
    depthwise = jnp.zeros_like(padded[1:-1, 1:-1, :])
    for offset_row in range(3):
        for offset_col in range(3):
            depthwise = (
                depthwise
                + kernel[3 * offset_row + offset_col]
                * padded[
                    offset_row : offset_row + size_cells, offset_col : offset_col + size_cells, :
                ]
            )
    centre_mean = jnp.mean(depthwise, axis=-1, keepdims=True)
    centred = depthwise - centre_mean
    spread = jnp.mean(centred * centred, axis=-1, keepdims=True)
    normed = centred * lax.rsqrt(spread + EPSILON) * gain_full
    flattened = normed.reshape(-1, normed.shape[-1])
    hidden = jax.nn.gelu(
        jnp.dot(flattened, up_full, precision=PRECISE, preferred_element_type=jnp.float32)
    )
    branch_out = jnp.dot(hidden, down_full, precision=PRECISE, preferred_element_type=jnp.float32)
    return padded[1:-1, 1:-1, :] + branch_out.reshape(depthwise.shape)


def trade_rims(
    low_strip, high_strip, partner, flip_codes, stride, low_edge, high_edge, low_border, high_border
):
    from_low = shifted(high_strip, "tile", stride)
    from_high = shifted(low_strip, "tile", -stride)
    pooled = lax.all_gather(jnp.stack([low_strip, high_strip]), "face", axis=0, tiled=True)
    face_count = pooled.shape[0] // 2
    pooled = pooled.reshape(face_count, 2, low_strip.shape[0], low_strip.shape[1])
    face_ids = jnp.arange(face_count, dtype=jnp.int32)
    pick_low = (face_ids == partner[low_edge]).astype(low_strip.dtype)
    pick_high = (face_ids == partner[high_edge]).astype(low_strip.dtype)
    seam_low = jnp.sum(pick_low[:, None, None] * pooled[:, 0], axis=0)
    seam_high = jnp.sum(pick_high[:, None, None] * pooled[:, 1], axis=0)
    seam_low = jnp.where(flip_codes[low_edge] == 1, seam_low[::-1], seam_low)
    seam_high = jnp.where(flip_codes[high_edge] == 1, seam_high[::-1], seam_high)
    return (jnp.where(low_border, seam_low, from_low), jnp.where(high_border, seam_high, from_high))


def pad_tile(own_tile, partner, flip_codes, tile_row, tile_col, grid_side):
    west_rim, east_rim = trade_rims(
        own_tile[:, 0],
        own_tile[:, -1],
        partner,
        flip_codes,
        1,
        2,
        3,
        tile_col == 0,
        tile_col == grid_side - 1,
    )
    widened = jnp.concatenate([west_rim[:, None], own_tile, east_rim[:, None]], axis=1)
    north_rim, south_rim = trade_rims(
        widened[0],
        widened[-1],
        partner,
        flip_codes,
        grid_side,
        0,
        1,
        tile_row == 0,
        tile_row == grid_side - 1,
    )
    return jnp.concatenate([north_rim[None], widened, south_rim[None]], axis=0)


def pad_adjoint(cotangent, partner, flip_codes, tile_row, tile_col, grid_side):
    back_north, back_south = trade_rims(
        cotangent[0],
        cotangent[-1],
        partner,
        flip_codes,
        grid_side,
        0,
        1,
        tile_row == 0,
        tile_row == grid_side - 1,
    )
    widened = cotangent[1:-1]
    widened = widened.at[0].add(back_north)
    widened = widened.at[-1].add(back_south)
    back_west, back_east = trade_rims(
        widened[:, 0],
        widened[:, -1],
        partner,
        flip_codes,
        1,
        2,
        3,
        tile_col == 0,
        tile_col == grid_side - 1,
    )
    interior = widened[:, 1:-1]
    interior = interior.at[:, 0].add(back_west)
    return interior.at[:, -1].add(back_east)


def shards(state_field, out_grad, depth_kernel, norm_gain, up_weight, down_weight, seam_code):
    own_tile = state_field[0, 0]
    tile_count = lax.axis_size("tile")
    face_total = lax.axis_size("face")
    grid_side = math.isqrt(tile_count)
    tile_index = lax.axis_index("tile")
    face_index = lax.axis_index("face")
    tile_row = tile_index // grid_side
    tile_col = tile_index % grid_side
    north_face = (face_index + face_total // 2) % face_total
    south_face = face_total - 1 - face_index
    west_face = jnp.where(
        face_index % 2 == 0, (face_index - 1) % face_total, (face_index + 1) % face_total
    )
    east_face = face_index ^ 1
    partner = jnp.stack([north_face, south_face, west_face, east_face])
    flip_codes = seam_code[0, 0]
    kernel, gain_full, up_full, down_full = (
        lax.all_gather(depth_kernel, "tile", axis=1, tiled=True),
        lax.all_gather(norm_gain, "tile", axis=0, tiled=True),
        lax.all_gather(up_weight, "tile", axis=0, tiled=True),
        lax.all_gather(down_weight, "tile", axis=0, tiled=True),
    )
    padded = pad_tile(own_tile, partner, flip_codes, tile_row, tile_col, grid_side)
    result, pull_back = jax.vjp(convnext_block, padded, kernel, gain_full, up_full, down_full)
    pad_grad, kernel_grad, gain_grad, up_grad, down_grad = pull_back(out_grad[0, 0])
    field_grad = pad_adjoint(pad_grad, partner, flip_codes, tile_row, tile_col, grid_side)
    shares = (
        lax.psum_scatter(kernel_grad, "tile", scatter_dimension=1, tiled=True),
        lax.psum_scatter(gain_grad, "tile", scatter_dimension=0, tiled=True),
        lax.psum_scatter(up_grad, "tile", scatter_dimension=0, tiled=True),
        lax.psum_scatter(down_grad, "tile", scatter_dimension=0, tiled=True),
    )
    kernel_part, gain_part, up_part, down_part = lax.psum(
        (shares[0], shares[1], shares[2], shares[3]), "face"
    )
    return (result[None, None], field_grad[None, None], kernel_part, gain_part, up_part, down_part)


def solution(mesh):
    placed = (
        P("face", "tile", None, None, None),
        P("face", "tile", None, None, None),
        P(None, "tile"),
        P("tile"),
        P("tile", None),
        P("tile", None),
        P("face", "tile", None),
    )
    return jax.shard_map(
        shards,
        mesh=mesh,
        in_specs=placed,
        out_specs=(
            P("face", "tile", None, None, None),
            P("face", "tile", None, None, None),
            P(None, "tile"),
            P("tile"),
            P("tile", None),
            P("tile", None),
        ),
        check_vma=False,
    )
```

profile of v0, /device:TPU:1, one launch (start us, length us, event | category | flops | bytes accessed | tf_op | source)
XLA Modules:
  0.0 1830.3 jit_solution(17901658781541039802)
XLA Ops:
  9.1 4.2 collective-permute-start
  13.3 1.3 collective-permute-start.1
  15.3 200.4 %all-gather = f32[64,4,9]{2,1,0:T(4,128)S(1)} all-gather(f32[1,4,9]{2,1,0:T(4,128)S(1)} %bitcast.216), channel_id=1, replica_groups=mesh['face'=8,'tile'=64] {'tile'}, dimensions={0}, use_global_device_ids=true | all-gather | bytes 9360 | tf_op jit(solution)/shard_map/all_gather | solution.py:136
  216.5 45.2 %all_gather.25 = f32[16,16,256]{2,1,0:T(8,128)S(1)} all-gather(f32[2,16,256]{2,1,0:T(8,128)S(1)} %pad_maximum_fusion.6), channel_id=1, replica_groups=mesh['face'=8,'tile'=64] {'face'}, dimensions={0}, use_global_device_ids=true | all-gather | bytes 294912 | tf_op jit(solution)/shard_map/all_gather | solution.py:47
  268.6 187.9 %all-reduce.19 = f32[256]{0:T(256)S(1)} all-reduce(f32[256]{0:T(256)S(1)} %dynamic-update-slice.13), channel_id=1, replica_groups=mesh['face'=8,'tile'=64] {'tile'}, use_global_device_ids=true, to_apply=%add.19 | all-reduce | flops 256 | bytes 2048
  456.7 1.3 collective-permute-start.2
  458.0 1.3 collective-permute-start.3
  459.4 42.3 %all_gather.26 = f32[16,18,256]{2,1,0:T(8,128)S(1)} all-gather(f32[2,18,256]{2,1,0:T(8,128)S(1)} %pad_maximum_fusion.4), channel_id=1, replica_groups=mesh['face'=8,'tile'=64] {'face'}, dimensions={0}, use_global_device_ids=true | all-gather | bytes 331776 | tf_op jit(solution)/shard_map/all_gather | solution.py:47
  504.0 1.7 reshape.283
  505.7 2.3 fusion.54
  508.0 2.6 fusion.5
  511.7 2.0 fusion.56
  513.7 2.5 fusion.7
  522.9 1.3 collective-permute-start.5
  524.2 8.8 collective-permute-start.4
  533.0 3.0 fusion.6
  537.4 378.2 %all-reduce.23 = (f32[9,256]{1,0:T(8,128)S(1)}, f32[256]{0:T(256)S(1)}) all-reduce(f32[9,256]{1,0:T(8,128)S(1)} %pad_add_fusion.5, f32[256]{0:T(256)S(1)} %copy-done.28), channel_id=2, replica_groups=mesh['face'=8,'tile'=64] {'tile'}, use_global_device_ids=true, to_apply=%region_21.22.clone | all-reduce | flops 2560 | bytes 20480
  915.8 66.3 %all_gather.30 = f32[16,18,256]{2,1,0:T(8,128)S(1)} all-gather(f32[2,18,256]{2,1,0:T(8,128)S(1)} %pad_maximum_fusion.5), channel_id=1, replica_groups=mesh['face'=8,'tile'=64] {'face'}, dimensions={0}, use_global_device_ids=true | all-gather | bytes 331776 | tf_op jit(solution)/shard_map/all_gather | solution.py:47
  982.7 1.3 collective-permute-start.6
  984.0 1.3 collective-permute-start.7
  985.3 14.3 all_gather.31
  1001.5 307.9 %all-reduce.27.cloned.1.call-done = f32[256,1024]{1,0:T(8,128)} async-done(((f32[256,1024]{1,0:T(8,128)}), f32[256,1024]{1,0:T(8,128)}) %all-reduce.27.cloned.1.call-update) | async-done | bytes 1048592
  1310.1 436.9 %reduce-scatter.3.cloned.1.call-done = f32[16,256]{1,0:T(8,128)} async-done(((f32[1024,256]{1,0:T(8,128)}), f32[16,256]{1,0:T(8,128)}) %reduce-scatter.3.cloned.1.call-update) | async-done | bytes 16400 | tf_op jit(solution)/shard_map/reduce_scatter | solution.py:149
  1747.0 76.1 %all-reduce.24 = (f32[9,4]{1,0:T(8,128)S(1)}, f32[4]{0:T(128)}, f32[4,1024]{1,0:T(4,128)}, f32[16,256]{1,0:T(8,128)}) all-reduce(f32[9,4]{1,0:T(8,128)S(1)} %constant_dynamic-slice_fusion.1, f32[4]{0:T(128)S(1)} %dynamic-slice.36, f32[4,1024]{1,0:T(4,128)S(1)} %constant_dynamic-slice_fusion, ...), channel_id=1, replica_groups=mesh['face'=8,'tile'=64] {'face'}, use_global_device_ids=true, to_apply=%region_22.23 | all-reduce | flops 8232 | bytes 65856 | tf_op jit(solution)/shard_map/psum | solution.py:151
  (169 shorter events, 21.4 us)
Async XLA Ops:
  7.2 496.8 %all-gather.7.cloned.1.call-start = ((), (), s32[]{:S(2)}) async-start(), calls=%async_computation.3 | async-start | bytes 1064960 | tf_op jit(solution)/shard_map/all_gather | solution.py:138
  7.9 497.8 %all-gather.5.cloned.1.call-start = ((), (), s32[]{:S(2)}) async-start(), calls=%async_computation.1 | async-start | bytes 1064960 | tf_op jit(solution)/shard_map/all_gather | solution.py:139
  9.1 207.3 %copy-start = (f32[1,1,16,16,256]{4,3,2,1,0:T(8,128)S(1)}, f32[1,1,16,16,256]{4,3,2,1,0:T(8,128)}, u32[]{:S(2)}) copy-start(f32[1,1,16,16,256]{4,3,2,1,0:T(8,128)} %param.15) | copy-start | bytes 786436
  9.1 447.4 %collective-permute-start = (f32[16,256]{1,0:T(8,128)S(1)}, f32[16,256]{1,0:T(8,128)S(1)}, u32[]{:S(2)}, u32[]{:S(2)}) collective-permute-start(f32[16,256]{1,0:T(8,128)S(1)} %get-tuple-element.127), channel_id=1, source_target_pairs={{0,1},{1,2},{2,3},{3,4},{4,5},{5,6},{6,7},{7,8},{8,9},{9,10},{10,1... | collective-permute-start | bytes 49160 | tf_op jit(solution)/shard_map/ppermute | solution.py:15
  13.3 443.2 %collective-permute-start.1 = (f32[16,256]{1,0:T(8,128)S(1)}, f32[16,256]{1,0:T(8,128)S(1)}, u32[]{:S(2)}, u32[]{:S(2)}) collective-permute-start(f32[16,256]{1,0:T(8,128)S(1)} %get-tuple-element.128), channel_id=1, source_target_pairs={{1,0},{2,1},{3,2},{4,3},{5,4},{6,5},{7,6},{8,7},{9,8},{10,9},{11,1... | collective-permute-start | bytes 49160 | tf_op jit(solution)/shard_map/ppermute | solution.py:15
  14.6 1294.8 %all-reduce.27.cloned.1.call-start = ((), (), s32[]{:S(2)}) async-start(), calls=%async_computation.4 | async-start | bytes 2097152
  215.8 243.5 %copy-start.9 = (f32[1,256]{1,0:T(1,128)}, f32[1,256]{1,0:T(1,128)S(1)}, u32[]{:S(2)}) copy-start(f32[1,256]{1,0:T(1,128)S(1)} %get-tuple-element.139) | copy-start | bytes 3076
  215.8 243.5 %copy-start.13 = (f32[1,256]{1,0:T(1,128)}, f32[1,256]{1,0:T(1,128)S(1)}, u32[]{:S(2)}) copy-start(f32[1,256]{1,0:T(1,128)S(1)} %get-tuple-element.141) | copy-start | bytes 3076
  215.9 286.3 %copy-start.15 = (f32[1,256]{1,0:T(1,128)}, f32[1,256]{1,0:T(1,128)S(1)}, u32[]{:S(2)}) copy-start(f32[1,256]{1,0:T(1,128)S(1)} %get-tuple-element.142) | copy-start | bytes 3076
  215.9 286.3 %copy-start.17 = (f32[1,256]{1,0:T(1,128)}, f32[1,256]{1,0:T(1,128)S(1)}, u32[]{:S(2)}) copy-start(f32[1,256]{1,0:T(1,128)S(1)} %get-tuple-element.143) | copy-start | bytes 3076
  215.9 286.4 %copy-start.7 = (f32[1,256]{1,0:T(1,128)}, f32[1,256]{1,0:T(1,128)S(1)}, u32[]{:S(2)}) copy-start(f32[1,256]{1,0:T(1,128)S(1)} %get-tuple-element.138) | copy-start | bytes 3076
  262.4 239.3 %copy-start.24 = (f32[8]{0:T(128)}, f32[8]{0:T(128)S(1)}, u32[]{:S(2)}) copy-start(f32[8]{0:T(128)S(1)} %get-tuple-element.154) | copy-start | bytes 100
  262.4 239.3 %copy-start.26 = (f32[8]{0:T(128)}, f32[8]{0:T(128)S(1)}, u32[]{:S(2)}) copy-start(f32[8]{0:T(128)S(1)} %get-tuple-element.155) | copy-start | bytes 100
  456.7 45.3 %collective-permute-start.2 = (f32[18,256]{1,0:T(8,128)S(1)}, f32[18,256]{1,0:T(8,128)S(1)}, u32[]{:S(2)}, u32[]{:S(2)}) collective-permute-start(f32[18,256]{1,0:T(8,128)S(1)} %get-tuple-element.112), channel_id=1, source_target_pairs={{0,8},{1,9},{2,10},{3,11},{4,12},{5,13},{6,14},{7,15},{8,16},{9,17... | collective-permute-start | bytes 55304 | tf_op jit(solution)/shard_map/ppermute | solution.py:15
  458.0 44.1 %collective-permute-start.3 = (f32[18,256]{1,0:T(8,128)S(1)}, f32[18,256]{1,0:T(8,128)S(1)}, u32[]{:S(2)}, u32[]{:S(2)}) collective-permute-start(f32[18,256]{1,0:T(8,128)S(1)} %get-tuple-element.113), channel_id=1, source_target_pairs={{8,0},{9,1},{10,2},{11,3},{12,4},{13,5},{14,6},{15,7},{16,8},{17,9... | collective-permute-start | bytes 55304 | tf_op jit(solution)/shard_map/ppermute | solution.py:15
  517.1 1229.9 %reduce-scatter.3.cloned.1.call-start = ((), (), s32[]{:S(2)}) async-start(), calls=%async_computation.2 | async-start | bytes 1064960 | tf_op jit(solution)/shard_map/reduce_scatter | solution.py:149
  522.9 459.5 %collective-permute-start.5 = (f32[18,256]{1,0:T(8,128)S(1)}, f32[18,256]{1,0:T(8,128)S(1)}, u32[]{:S(2)}, u32[]{:S(2)}) collective-permute-start(f32[18,256]{1,0:T(8,128)S(1)} %get-tuple-element.102), channel_id=1, source_target_pairs={{8,0},{9,1},{10,2},{11,3},{12,4},{13,5},{14,6},{15,7},{16,8},{17,9... | collective-permute-start | bytes 55304 | tf_op jit(solution)/shard_map/ppermute | solution.py:15
  524.2 458.2 %collective-permute-start.4 = (f32[18,256]{1,0:T(8,128)S(1)}, f32[18,256]{1,0:T(8,128)S(1)}, u32[]{:S(2)}, u32[]{:S(2)}) collective-permute-start(f32[18,256]{1,0:T(8,128)S(1)} %get-tuple-element.103), channel_id=1, source_target_pairs={{0,8},{1,9},{2,10},{3,11},{4,12},{5,13},{6,14},{7,15},{8,16},{9,17... | collective-permute-start | bytes 55304 | tf_op jit(solution)/shard_map/ppermute | solution.py:15
  915.7 66.3 %copy-start.25 = (f32[8]{0:T(128)S(1)}, f32[8]{0:T(128)}, u32[]{:S(2)}) copy-start(f32[8]{0:T(128)} %copy-done.24) | copy-start | bytes 100
  915.7 66.3 %copy-start.27 = (f32[8]{0:T(128)S(1)}, f32[8]{0:T(128)}, u32[]{:S(2)}) copy-start(f32[8]{0:T(128)} %copy-done.26) | copy-start | bytes 100
  915.8 66.6 %copy-start.2 = (f32[18,18,256]{2,1,0:T(8,128)S(1)}, f32[18,18,256]{2,1,0:T(8,128)}, u32[]{:S(2)}) copy-start(f32[18,18,256]{2,1,0:T(8,128)} %copy-done.1) | copy-start | bytes 995332
  915.8 66.6 %slice-start = ((f32[18,18,256]{2,1,0:T(8,128)}), f32[16,18,256]{2,1,0:T(8,128)S(1)}, s32[]{:S(2)}) async-start(f32[18,18,256]{2,1,0:T(8,128)} %copy-done.1), calls=%async_computation.5 | async-start | bytes 786432 | tf_op jit(solution)/shard_map/slice | solution.py:99
  982.7 17.8 collective-permute-start.6
  984.0 16.6 collective-permute-start.7
  (26 other events, 48.1 us)
Sparse Core Ops, SparseCore 0:
  12.5 131.3 all-gather.6
  148.4 123.8 all-gather.4
  517.2 792.1 all-reduce.26
  1312.2 434.7 reduce-scatter.2
where the time goes:
time: 1830 us
  blocking collectives  1010 us (55%)
  waiting for transfers between devices  746 us (41%)
  starting transfers between devices  21.1 us (1%)
  between operations  18.6 us (1%)
    unnamed x2, blocking collectives  566 us
    reduce_scatter x1, waiting for transfers between devices, shards(): lax.psum_scatter(down_grad, 'tile', scatter_dimension=0, tiled=True)  437 us
    unnamed x5, waiting for transfers between devices  309 us
    all_gather x1, blocking collectives, shards(): lax.all_gather(depth_kernel, 'tile', axis=1, tiled=True)  200 us
    all_gather x4, blocking collectives, trade_rims(): lax.all_gather(jnp.stack([low_strip, high_strip]), 'face', axis=0, tiled=...  168 us
    psum x1, blocking collectives, shards(): lax.psum((shares[0], shares[1], shares[2], shares[3]), 'face')  76.1 us
  transfers between devices with their start and end apart: 12, of which 2 were waited for; matrix products, arithmetic and copies ran while one was open for 1% of the time, Pallas kernels for 0%

commit v1 on v0

v1 whole, which is shorter than its diff:
```python
import functools
import math

import jax
import jax.numpy as jnp
from jax import lax
from jax.experimental import pallas as pl
from jax.experimental.pallas import tpu as pltpu
from jax.sharding import PartitionSpec as P

EPSILON = 1e-06
NX, NH, NY, NL, NC = 4, 2, 8, 4, 2
MESH = pl.DeviceIdType.MESH
F32, BF16 = jnp.float32, jnp.bfloat16
ROOT = math.sqrt(2.0 / math.pi)
NN = (((1,), (0,)), ((), ()))
NT = (((1,), (1,)), ((), ()))


class Slots:
    def __init__(self):
        self.used = 0

    def take(self, count):
        first = self.used
        self.used += count
        return first


SLOTS = Slots()
S_XH = SLOTS.take(8)
S_RING = SLOTS.take(32)
S_X = SLOTS.take(24)
S_SIB = SLOTS.take(8)
S_KG1 = SLOTS.take(8)
S_KG2 = SLOTS.take(8)
S_HALO = SLOTS.take(4)
R_SIB = SLOTS.take(8)
R_RING = SLOTS.take(32)
R_X = SLOTS.take(24)
R_Z = SLOTS.take(8)
R_F = SLOTS.take(8)
R_KY = SLOTS.take(8)
R_KX = SLOTS.take(4)
R_KZ = SLOTS.take(16)
R_HALO = SLOTS.take(4)
N_SLOTS = SLOTS.used

SIGNS = ((0, 1), (0, -1))


def split(value):
    high = value.astype(BF16)
    return high, (value - high.astype(F32)).astype(BF16)


def dot3(a, b, dims):
    def one(p, q):
        return lax.dot_general(p, q, dims, preferred_element_type=F32)

    return one(a[0], b[0]) + (one(a[0], b[1]) + one(a[1], b[0]))


def device(x, h, y, l, c):
    return (l * NC + c, (x * NH + h) * NY + y)


def kernel(
    state, cot, up, down, kg, code,
    out_new, out_field, out_up, out_down, out_kg,
    w, g, padded, pgrad, zpad, ns_send, ns_recv, we_send, we_recv, bns_send, bns_recv, bwe_send, bwe_recv,
    kg_own, kg_xh, kg_all, kgr_own, kgr_y, kgr_x, kgr_z,
    u_hi, u_lo, d_hi, d_lo, xhat, rstd, n_hi, n_lo, nt_hi, nt_lo, g_hi, g_lo, branch, dnorm, ugrad, ddw, krows,
    s_recv, ring_recv0, ring_recv1, x_recv0, x_recv1, z_recv, final,
    ssem, rsem,
):
    face, tile = lax.axis_index("face"), lax.axis_index("tile")
    l, c = face // 2, face % 2
    x, h, y = tile // 16, (tile // 8) % 2, tile % 8
    xh = x * 2 + h
    z = h * 4 + l

    def copy(src, dst, slot, to):
        return pltpu.make_async_remote_copy(
            src_ref=src, dst_ref=dst, send_sem=ssem.at[slot], recv_sem=rsem.at[slot],
            device_id=to, device_id_type=MESH,
        )

    def arrived(dst, slot):
        copy(dst, dst, slot, device(x, h, y, l, 1 - c)).wait_recv()

    barrier = pltpu.get_barrier_semaphore()
    peers = []
    for k in range(1, 16):
        peers.append(device(x, (h + k // 8) % 2, y, (l + (k // 2) % 4) % 4, (c + k % 2) % 2))
    for k in range(1, NY):
        peers.append(device(x, h, (y + k) % NY, l, c))
    for dx in range(1, NX):
        for dh in range(NH):
            peers.append(device((x + dx) % NX, (h + dh) % NH, y, l, c))
    for peer in peers:
        pl.semaphore_signal(barrier, inc=1, device_id=peer, device_id_type=MESH)

    sub8 = lax.broadcasted_iota(jnp.int32, (8, 128), 0)

    def own_blocks(core):
        for q in range(2):
            lanes = slice(256 * core + 128 * q, 256 * core + 128 * q + 128)
            lanes2 = slice(512 + 256 * core + 128 * q, 512 + 256 * core + 128 * q + 128)
            w[core, y, xh * 4 + q] = jnp.concatenate([up[:, lanes], up[:, lanes2]], axis=0)
            w[core, y, xh * 4 + 2 + q] = down[8 * core : 8 * core + 8, 128 * q : 128 * q + 128]

    for core in range(2):
        pl.when(c == core)(functools.partial(own_blocks, core))
    kg_tile = jnp.where(sub8 == xh, jnp.broadcast_to(kg[...], (8, 128)), 0.0)
    kg_own[...] = kg_tile
    kg_xh[0] = kg_tile

    flips = [code[0, e].astype(F32) for e in range(4)]

    def mixed(flip, a, b):
        return a * (1.0 - flip) + b * flip

    for i in range(16):
        padded[1 + i, 8:24, :] = state[i]
        we_send[0, i : i + 1, :] = mixed(flips[2], state[i, 0:1, :], state[15 - i, 0:1, :])
        we_send[1, i : i + 1, :] = mixed(flips[3], state[i, 15:16, :], state[15 - i, 15:16, :])

    row, col = xh, y
    inner_n, inner_s = (row + 7) // 8, (14 - row) // 8
    inner_w, inner_e = (col + 7) // 8, (14 - col) // 8
    across = (
        (face + 4) % 8,
        7 - face,
        (face + 7 + 2 * (face % 2)) % 8,
        face + 1 - 2 * (face % 2),
    )

    def rim_copies(send, recv, base, stride, low_edge, high_edge, inner_low, inner_high):
        low_to = (
            inner_low * face + (1 - inner_low) * across[low_edge],
            tile - stride * inner_low,
        )
        high_to = (
            inner_high * face + (1 - inner_high) * across[high_edge],
            tile + stride * inner_high,
        )
        low = pltpu.make_async_remote_copy(
            src_ref=send.at[0], dst_ref=recv.at[inner_low], send_sem=ssem.at[base],
            recv_sem=rsem.at[base + inner_low], device_id=low_to, device_id_type=MESH,
        )
        high = pltpu.make_async_remote_copy(
            src_ref=send.at[1], dst_ref=recv.at[1 - inner_high], send_sem=ssem.at[base + 1],
            recv_sem=rsem.at[base + 1 - inner_high], device_id=high_to, device_id_type=MESH,
        )
        return low, high

    pl.semaphore_wait(barrier, len(peers))

    we = rim_copies(we_send, we_recv, S_HALO, 1, 2, 3, inner_w, inner_e)
    for each in we:
        each.start()
    kg1 = []
    for k in range(1, 8):
        dx, dh = k // 2, k % 2
        kg1.append(
            copy(kg_own, kg_xh.at[k], S_KG1 + k, device((x + dx) % NX, (h + dh) % NH, y, l, c))
        )

    def own_chunk(core, xs, hs):
        return w.at[core, y, pl.ds((xs * 2 + hs) * 4, 4)]

    def first_leg_0():
        mine = own_chunk(0, x, h)
        for k in (1, 2, 6, 3, 7, 4, 5):
            dx, dh = k // 2, k % 2
            copy(mine, mine, S_XH + k, device((x + dx) % NX, (h + dh) % NH, y, l, c)).start()

    def first_leg_1():
        mine = own_chunk(1, x, h)
        copy(mine, mine, S_XH + 1, device(x, 1 - h, y, l, c)).start()

    pl.when(c == 0)(first_leg_0)
    pl.when(c == 1)(first_leg_1)
    for each in kg1:
        each.start()

    for k in range(2):
        arrived(we_recv.at[k], S_HALO + k)
    for i in range(16):
        padded[1 + i, 7:8, :] = we_recv[0, i : i + 1, :]
        padded[1 + i, 24:25, :] = we_recv[1, i : i + 1, :]
    for i in range(18):
        ns_send[0, i : i + 1, :] = mixed(flips[0], padded[1, 7 + i : 8 + i, :], padded[1, 24 - i : 25 - i, :])
        ns_send[1, i : i + 1, :] = mixed(flips[1], padded[16, 7 + i : 8 + i, :], padded[16, 24 - i : 25 - i, :])
    ns = rim_copies(ns_send, ns_recv, S_HALO + 2, 8, 0, 1, inner_n, inner_s)
    for each in ns:
        each.start()
    for k in range(1, 8):
        arrived(kg_xh.at[k], S_KG1 + k)
    total = kg_xh[0]
    for k in range(1, 8):
        total = total + kg_xh[k]
    kg_all[y] = total
    kg2 = []
    for k in range(1, NY):
        mine = kg_all.at[y]
        each = copy(mine, mine, S_KG2 + k, device(x, h, (y + k) % NY, l, c))
        each.start()
        kg2.append(each)

    sibling = device(x, h, y, l, 1 - c)
    near = [0, -1, 1, -2, 2, -3, 3, 4]

    def ring_to(sign):
        return device(x, h, (y + sign + NY) % NY, l, c)

    def gather_0():
        sends = []

        def sub(yy, dx):
            return w.at[0, yy, pl.ds(((x - dx + NX) % NX) * 8, 8)]

        def hop(way, step, dx):
            sign = 1 if way == 0 else -1
            ref = sub((y - sign * step + NY) % NY, dx)
            each = copy(ref, ref, S_RING + way * 16 + step * 4 + dx, ring_to(sign))
            each.start()
            sends.append(each)

        for dx in range(NX):
            for dh in range(NH):
                if dx or dh:
                    arrived(own_chunk(0, (x - dx + NX) % NX, (h - dh + NH) % NH), S_XH + dx * 2 + dh)
            hop(0, 0, dx)
            hop(1, 0, dx)
        sib = copy(w.at[0, y], w.at[0, y], S_SIB, sibling)
        sib.start()
        sends.append(sib)
        for step in range(1, 5):
            for dx in range(NX):
                for way in range(2):
                    if step == 4 and (dx // 2) != way:
                        continue
                    sign = 1 if way == 0 else -1
                    arrived(sub((y - sign * step + NY) % NY, dx), S_RING + way * 16 + (step - 1) * 4 + dx)
                    if step < 3 or (step == 3 and (dx // 2) == way):
                        hop(way, step, dx)
            for offset in (-step, step) if step < 4 else (4,):
                ref = w.at[0, (y + offset + NY) % NY]
                sib = copy(ref, ref, S_SIB + near.index(offset), sibling)
                sib.start()
                sends.append(sib)
        mine = own_chunk(0, x, h)
        for k in range(1, 8):
            sends.append(copy(mine, mine, S_XH + k, sibling))
        for each in sends:
            each.wait_send()

    def gather_1():
        sends = []

        def sub(yy, hs):
            return w.at[1, yy, pl.ds(x * 8 + hs * 4, 4)]

        def hop(way, step, hs):
            sign = 1 if way == 0 else -1
            ref = sub((y - sign * step + NY) % NY, hs)
            each = copy(ref, ref, S_RING + way * 16 + step * 4 + hs, ring_to(sign))
            each.start()
            sends.append(each)

        def spread(offset):
            ref = w.at[1, (y + offset + NY) % NY, pl.ds(x * 8, 8)]
            for dx in (2, 1, 3):
                each = copy(
                    ref, ref, S_X + (dx - 1) * 8 + near.index(offset), device((x + dx) % NX, h, y, l, c)
                )
                each.start()
                sends.append(each)

        arrived(own_chunk(1, x, 1 - h), S_XH + 1)
        for hs in range(2):
            hop(0, 0, hs)
            hop(1, 0, hs)
        spread(0)
        for step in range(1, 5):
            for hs in range(2):
                for way in range(2):
                    if step == 4 and hs != way:
                        continue
                    sign = 1 if way == 0 else -1
                    arrived(sub((y - sign * step + NY) % NY, hs), S_RING + way * 16 + (step - 1) * 4 + hs)
                    if step < 3 or (step == 3 and hs == way):
                        hop(way, step, hs)
            for offset in (-step, step) if step < 4 else (4,):
                spread(offset)
        for offset in near:
            yy = (y + offset + NY) % NY
            for dx in range(1, NX):
                arrived(w.at[1, yy, pl.ds(((x - dx + NX) % NX) * 8, 8)], S_X + (dx - 1) * 8 + near.index(offset))
            sib = copy(w.at[1, yy], w.at[1, yy], S_SIB + near.index(offset), sibling)
            sib.start()
            sends.append(sib)
        mine = own_chunk(1, x, h)
        sends.append(copy(mine, mine, S_XH + 1, sibling))
        for each in sends:
            each.wait_send()

    pl.when(c == 0)(gather_0)
    pl.when(c == 1)(gather_1)

    for k in range(1, NY):
        ref = kg_all.at[(y - k + NY) % NY]
        arrived(ref, S_KG2 + k)
    rows64 = lax.broadcasted_iota(jnp.int32, (64, 256), 0)
    chan = lax.broadcasted_iota(jnp.int32, (64, 256), 1)
    owner = (chan // 4) == ((rows64 % 8) * 8 + rows64 // 8)
    lane = lax.broadcasted_iota(jnp.int32, (64, 128), 1)
    same4 = (
        lax.broadcasted_iota(jnp.int32, (128, 256), 0) % 4
        == lax.broadcasted_iota(jnp.int32, (128, 256), 1) % 4
    )
    spread4 = jnp.where(same4, 1.0, 0.0).astype(BF16)
    tiles = kg_all[...].reshape(64, 128)
    grouped = jnp.concatenate(
        [jnp.where(lane // 4 == k, tiles, 0.0) for k in range(10)], axis=0
    )
    first, second = split(grouped)
    spread_rows = lax.dot_general(first, spread4, NN, preferred_element_type=F32) + lax.dot_general(
        second, spread4, NN, preferred_element_type=F32
    )
    for k in range(10):
        krows[k : k + 1, :] = jnp.sum(
            jnp.where(owner, spread_rows[64 * k : 64 * k + 64], 0.0), axis=0, keepdims=True
        )

    for k in range(2):
        arrived(ns_recv.at[k], S_HALO + 2 + k)
    padded[0, 7:25, :] = ns_recv[0]
    padded[17, 7:25, :] = ns_recv[1]

    gain = krows[9:10, :]

    def conv_row(r, carry):
        acc = jnp.zeros((16, 256), F32)
        for i in range(3):
            for j in range(3):
                acc = acc + krows[3 * i + j : 3 * i + j + 1, :] * padded[r + i, 7 + j : 23 + j, :]
        mean = jnp.mean(acc, axis=-1, keepdims=True)
        centred = acc - mean
        var = jnp.mean(centred * centred, axis=-1, keepdims=True)
        inv = lax.rsqrt(var + EPSILON)
        hat = centred * inv
        at = pl.ds(pl.multiple_of(r * 16, 16), 16)
        xhat[at, :] = hat
        rstd[at, :] = jnp.broadcast_to(inv, (16, 128))
        high, low = split(hat * gain)
        n_hi[at, :] = high
        n_lo[at, :] = low
        high, low = split(cot[r])
        g_hi[at, :] = high
        g_lo[at, :] = low
        return carry

    lax.fori_loop(0, 16, conv_row, 0)
    high, low = split(jnp.transpose(xhat[...] * gain))
    nt_hi[...] = high
    nt_lo[...] = low

    for k, offset in enumerate(near):
        arrived(w.at[1 - c, (y + offset + NY) % NY], S_SIB + k)

    lows = lax.broadcasted_iota(jnp.int32, (4, 8, 128), 1) < 4

    def unpack(xs, carry):
        for hs in range(NH):
            for q in range(2):
                ref = pl.ds(xs * 8 + hs * 4 + q, 1)
                for cc in range(2):
                    v = w[cc, :, ref].reshape(4, 2, 8, 128)
                    a, b = v[:, 0], v[:, 1]
                    at = pl.ds(pl.multiple_of(xs * 64 + hs * 32, 32), 32)
                    for half, value in (
                        (0, jnp.where(lows, a, pltpu.roll(b, 4, 1))),
                        (1, jnp.where(lows, pltpu.roll(a, 4, 1), b)),
                    ):
                        high, low = split(value.reshape(32, 128))
                        u_hi[2 * half + cc, at, 128 * q : 128 * q + 128] = high
                        u_lo[2 * half + cc, at, 128 * q : 128 * q + 128] = low
                ref = pl.ds(xs * 8 + hs * 4 + 2 + q, 1)
                both = jnp.concatenate(
                    [w[0, :, ref].reshape(8, 8, 128), w[1, :, ref].reshape(8, 8, 128)], axis=1
                ).reshape(128, 128)
                high, low = split(both)
                d_hi[xs, 128 * hs : 128 * hs + 128, 128 * q : 128 * q + 128] = high
                d_lo[xs, 128 * hs : 128 * hs + 128, 128 * q : 128 * q + 128] = low
        return carry

    lax.fori_loop(0, NX, unpack, 0)

    branch[...] = jnp.zeros_like(branch)
    dnorm[...] = jnp.zeros_like(dnorm)

    def chunk(j, carry):
        normed = (n_hi[...], n_lo[...])
        grads = (g_hi[...], g_lo[...])
        ups = (u_hi[j], u_lo[j])
        downs = (d_hi[j], d_lo[j])
        pre = dot3(normed, ups, NN)
        back = dot3(grads, downs, NT)
        square = pre * pre
        t = jnp.tanh(ROOT * (pre + 0.044715 * (square * pre)))
        half = 0.5 * (1.0 + t)
        hidden = pre * half
        slope = half + 0.5 * pre * (1.0 - t * t) * (ROOT * (1.0 + 3 * 0.044715 * square))
        dpre = back * slope
        branch[...] += dot3(split(hidden), downs, NN)
        dp = split(dpre)
        dnorm[...] += dot3(dp, ups, NT)
        ugrad[j] = dot3((nt_hi[...], nt_lo[...]), dp, NN)
        dg = dot3(split(jnp.transpose(hidden)), grads, NN)
        for hs in range(NH):
            for q in range(2):
                v = dg[128 * hs : 128 * hs + 128, 128 * q : 128 * q + 128].reshape(8, 2, 8, 128)
                for cc in range(2):
                    g[cc, :, pl.ds(j * 8 + hs * 4 + 2 + q, 1)] = v[:, cc].reshape(8, 1, 8, 128)
        return carry

    lax.fori_loop(0, 4, chunk, 0)

    def pack(xs, carry):
        for hs in range(NH):
            for q in range(2):
                for cc in range(2):
                    at = pl.ds(pl.multiple_of(xs * 64 + hs * 32, 32), 32)
                    v0 = ugrad[cc, at, 128 * q : 128 * q + 128].reshape(4, 8, 128)
                    v1 = ugrad[2 + cc, at, 128 * q : 128 * q + 128].reshape(4, 8, 128)
                    even = jnp.where(lows, v0, pltpu.roll(v1, 4, 1))
                    odd = jnp.where(lows, pltpu.roll(v0, 4, 1), v1)
                    both = jnp.concatenate([even[:, None], odd[:, None]], axis=1)
                    g[cc, :, pl.ds(xs * 8 + hs * 4 + q, 1)] = both.reshape(8, 1, 8, 128)
        return carry

    lax.fori_loop(0, NX, pack, 0)

    far = [4, 3, -3, 2, -2, 1, -1, 0]
    swaps = []
    for k, offset in enumerate(far):
        yy = (y + offset + NY) % NY
        each = copy(g.at[1 - c, yy], s_recv.at[yy], R_SIB + k, sibling)
        each.start()
        swaps.append(each)

    for r in range(16):
        out_new[r] = state[r] + branch[16 * r : 16 * r + 16, :]

    krows[9:10, :] = jnp.sum(dnorm[...] * xhat[...], axis=0, keepdims=True)
    zpad[...] = jnp.zeros_like(zpad)

    def norm_row(r, sums):
        at = pl.ds(pl.multiple_of(r * 16, 16), 16)
        hat = xhat[at, :]
        inv = rstd[at, :][:, 0:1]
        dhat = dnorm[at, :] * gain
        mean = jnp.mean(dhat, axis=-1, keepdims=True)
        cross = jnp.mean(dhat * hat, axis=-1, keepdims=True)
        dd = inv * (dhat - mean - hat * cross)
        zpad[r + 2, 8:24, :] = dd
        fresh = []
        for i in range(3):
            for j in range(3):
                v = dd * padded[r + i, 7 + j : 23 + j, :]
                fresh.append(sums[3 * i + j] + v[0:8] + v[8:16])
        return tuple(fresh)

    gain_saved = gain
    sums = lax.fori_loop(0, 16, norm_row, tuple(jnp.zeros((8, 256), F32) for _ in range(9)))
    kernel_rows = [krows[k : k + 1, :] for k in range(9)]

    def back_row(r, carry):
        acc = jnp.zeros((18, 256), F32)
        for i in range(3):
            for j in range(3):
                acc = acc + krows[3 * i + j : 3 * i + j + 1, :] * zpad[r + 2 - i, 8 - j : 26 - j, :]
        pgrad[r, 7:25, :] = acc
        return carry

    lax.fori_loop(0, 18, back_row, 0)
    for i in range(18):
        bns_send[0, i : i + 1, :] = mixed(flips[0], pgrad[0, 7 + i : 8 + i, :], pgrad[0, 24 - i : 25 - i, :])
        bns_send[1, i : i + 1, :] = mixed(flips[1], pgrad[17, 7 + i : 8 + i, :], pgrad[17, 24 - i : 25 - i, :])
    bns = rim_copies(bns_send, bns_recv, R_HALO, 8, 0, 1, inner_n, inner_s)
    for each in bns:
        each.start()

    grad_rows = [jnp.sum(sums[k], axis=0, keepdims=True) for k in range(9)] + [krows[9:10, :]]
    grouped = jnp.concatenate([jnp.where(owner, jnp.broadcast_to(v, (64, 256)), 0.0) for v in grad_rows], axis=0)
    first, second = split(grouped)
    fold = lax.dot_general(first, spread4, NT, preferred_element_type=F32) + lax.dot_general(
        second, spread4, NT, preferred_element_type=F32
    )
    folded = jnp.zeros((64, 128), F32)
    for k in range(10):
        folded = folded + jnp.where(lane // 4 == k, fold[64 * k : 64 * k + 64], 0.0)
    kgr_own[...] = folded.reshape(8, 8, 128)
    kgs = []
    for k in range(1, NY):
        yy = (y + k) % NY
        each = copy(kgr_own.at[yy], kgr_y.at[k], R_KY + k, device(x, h, yy, l, c))
        each.start()
        kgs.append(each)

    def add(dst, src):
        dst[...] = dst[...] + src[...]

    def swapped(offset):
        yy = (y + offset + NY) % NY
        arrived(s_recv.at[yy], R_SIB + far.index(offset))
        return yy

    def reduce_0():
        sends = []

        def sub(offset, xs):
            return g.at[0, (y + offset + NY) % NY, pl.ds(xs * 8, 8)]

        def hop(way, step, xs):
            sign = 1 if way == 0 else -1
            each = copy(
                sub(sign * (4 - step), xs), ring_recv0.at[way, step, xs],
                R_RING + way * 16 + step * 4 + xs, ring_to(sign),
            )
            each.start()
            sends.append(each)

        for step in range(4):
            for offset in (4,) if step == 0 else (4 - step, step - 4):
                yy = swapped(offset)
                add(g.at[0, yy], s_recv.at[yy])
            for xs in range(NX):
                for way in range(2):
                    sign = 1 if way == 0 else -1
                    started = (xs // 2) == way
                    if step == 0 and not started:
                        continue
                    if step > 1 or (step == 1 and started):
                        arrived(ring_recv0.at[way, step - 1, xs], R_RING + way * 16 + (step - 1) * 4 + xs)
                        add(sub(sign * (4 - step), xs), ring_recv0.at[way, step - 1, xs])
                    hop(way, step, xs)
        yy = swapped(0)
        add(g.at[0, yy], s_recv.at[yy])
        for way in range(2):
            for xs in range(NX):
                arrived(ring_recv0.at[way, 3, xs], R_RING + way * 16 + 12 + xs)
                add(sub(0, xs), ring_recv0.at[way, 3, xs])
        for dx in (2, 1, 3):
            to = (x + dx) % NX
            each = copy(sub(0, to), x_recv0.at[dx - 1], R_X + dx - 1, device(to, h, y, l, c))
            each.start()
            sends.append(each)
        for dx in (1, 3, 2):
            arrived(x_recv0.at[dx - 1], R_X + dx - 1)
            add(sub(0, x), x_recv0.at[dx - 1])
        for each in sends:
            each.wait_send()

    def reduce_1():
        sends = []

        def block(offset, xs):
            return g.at[1, (y + offset + NY) % NY, pl.ds(xs * 8, 8)]

        def sub(offset, hs):
            return g.at[1, (y + offset + NY) % NY, pl.ds(x * 8 + hs * 4, 4)]

        for k, offset in enumerate(far):
            yy = swapped(offset)
            add(g.at[1, yy], s_recv.at[yy])
            for dx in (2, 1, 3):
                to = (x + dx) % NX
                each = copy(
                    block(offset, to), x_recv1.at[k, dx - 1], R_X + (dx - 1) * 8 + k, device(to, h, y, l, c)
                )
                each.start()
                sends.append(each)

        def hop(way, step, hs):
            sign = 1 if way == 0 else -1
            each = copy(
                sub(sign * (4 - step), hs), ring_recv1.at[way, step, hs],
                R_RING + way * 16 + step * 4 + hs, ring_to(sign),
            )
            each.start()
            sends.append(each)

        def gathered(offset):
            k = far.index(offset)
            for dx in (1, 3, 2):
                arrived(x_recv1.at[k, dx - 1], R_X + (dx - 1) * 8 + k)
                add(block(offset, x), x_recv1.at[k, dx - 1])

        for step in range(4):
            for offset in (4,) if step == 0 else (4 - step, step - 4):
                gathered(offset)
            for hs in range(2):
                for way in range(2):
                    sign = 1 if way == 0 else -1
                    started = hs == way
                    if step == 0 and not started:
                        continue
                    if step > 1 or (step == 1 and started):
                        arrived(ring_recv1.at[way, step - 1, hs], R_RING + way * 16 + (step - 1) * 4 + hs)
                        add(sub(sign * (4 - step), hs), ring_recv1.at[way, step - 1, hs])
                    hop(way, step, hs)
        gathered(0)
        for way in range(2):
            for hs in range(2):
                arrived(ring_recv1.at[way, 3, hs], R_RING + way * 16 + 12 + hs)
                add(sub(0, hs), ring_recv1.at[way, 3, hs])
        for each in sends:
            each.wait_send()

    pl.when(c == 0)(reduce_0)
    pl.when(c == 1)(reduce_1)

    ends = []

    def piece(hs, ls):
        return g.at[c, y, x * 8 + hs * 4 + ls]

    for k in range(1, 8):
        zz = (z + k) % 8
        each = copy(piece(zz // 4, zz % 4), z_recv.at[k], R_Z + k, device(x, zz // 4, y, zz % 4, c))
        each.start()
        ends.append(each)

    for k in range(2):
        arrived(bns_recv.at[k], R_HALO + k)
    pgrad[1, 7:25, :] = pgrad[1, 7:25, :] + bns_recv[0]
    pgrad[16, 7:25, :] = pgrad[16, 7:25, :] + bns_recv[1]
    for i in range(16):
        bwe_send[0, i : i + 1, :] = mixed(flips[2], pgrad[1 + i, 7:8, :], pgrad[16 - i, 7:8, :])
        bwe_send[1, i : i + 1, :] = mixed(flips[3], pgrad[1 + i, 24:25, :], pgrad[16 - i, 24:25, :])
    bwe = rim_copies(bwe_send, bwe_recv, R_HALO + 2, 1, 2, 3, inner_w, inner_e)
    for each in bwe:
        each.start()

    for k in range(1, NY):
        arrived(kgr_y.at[k], R_KY + k)
    total = kgr_own[y]
    for k in range(1, NY):
        total = total + kgr_y[k]
    kgr_x[x] = total
    for k in range(1, NX):
        to = (x + k) % NX
        each = copy(kgr_x.at[x], kgr_x.at[x], R_KX + k, device(to, h, y, l, c))
        each.start()
        kgs.append(each)

    total = piece(h, l)[...]
    for k in range(1, 8):
        arrived(z_recv.at[k], R_Z + k)
        total = total + z_recv[k]
    final[c, l] = total
    for k in range(1, 8):
        ll, cc = (l + k // 2) % 4, (c + k % 2) % 2
        each = copy(final.at[c, l], final.at[c, l], R_F + k, device(x, h, y, ll, cc))
        each.start()
        ends.append(each)

    for k in range(1, NX):
        arrived(kgr_x.at[(x - k + NX) % NX], R_KX + k)
    total = kgr_x[0]
    for k in range(1, NX):
        total = total + kgr_x[k]
    zc = z * 2 + c
    kgr_z[zc] = total
    for k in range(1, 16):
        to = device(x, (h + k // 8) % 2, y, (l + (k // 2) % 4) % 4, (c + k % 2) % 2)
        each = copy(kgr_z.at[zc], kgr_z.at[zc], R_KZ + k, to)
        each.start()
        kgs.append(each)

    for k in range(2):
        arrived(bwe_recv.at[k], R_HALO + 2 + k)
    for i in range(16):
        pgrad[1 + i, 8:9, :] = pgrad[1 + i, 8:9, :] + bwe_recv[0, i : i + 1, :]
        pgrad[1 + i, 23:24, :] = pgrad[1 + i, 23:24, :] + bwe_recv[1, i : i + 1, :]
        out_field[i] = pgrad[1 + i, 8:24, :] + cot[i]

    for k in range(1, 8):
        ll, cc = (l - k // 2 + 4) % 4, (c + k % 2) % 2
        arrived(final.at[cc, ll], R_F + k)
    for cc in range(2):
        for q in range(2):
            v = final[cc, q]
            out_up[:, 256 * cc + 128 * q : 256 * cc + 128 * q + 128] = v[0:4]
            out_up[:, 512 + 256 * cc + 128 * q : 512 + 256 * cc + 128 * q + 128] = v[4:8]
            out_down[8 * cc : 8 * cc + 8, 128 * q : 128 * q + 128] = final[cc, 2 + q]

    for k in range(1, 16):
        hh, ll, cc = (h + k // 8) % 2, (l - (k // 2) % 4 + 4) % 4, (c + k % 2) % 2
        arrived(kgr_z.at[(hh * 4 + ll) * 2 + cc], R_KZ + k)
    total = kgr_z[0]
    for k in range(1, 16):
        total = total + kgr_z[k]
    out_kg[...] = jnp.sum(jnp.where(sub8 == xh, total, 0.0), axis=0, keepdims=True)

    for each in [*we, *kg1, *ns, *kg2, *swaps, *bns, *kgs, *bwe, *ends]:
        each.wait_send()


def shards(state_field, out_grad, depth_kernel, norm_gain, up_weight, down_weight, seam_code):
    kg = jnp.concatenate([depth_kernel.reshape(1, 36), norm_gain.reshape(1, 4), jnp.zeros((1, 88), F32)], axis=1)
    vmem = pl.BlockSpec(memory_space=pltpu.VMEM)

    def buf(*shape, dtype=F32):
        return pltpu.VMEM(shape, dtype)

    new, field, up, down, kgo = pl.pallas_call(
        kernel,
        out_shape=(
            jax.ShapeDtypeStruct((16, 16, 256), F32),
            jax.ShapeDtypeStruct((16, 16, 256), F32),
            jax.ShapeDtypeStruct((4, 1024), F32),
            jax.ShapeDtypeStruct((16, 256), F32),
            jax.ShapeDtypeStruct((1, 128), F32),
        ),
        in_specs=[vmem] * 5 + [pl.BlockSpec(memory_space=pltpu.SMEM)],
        out_specs=(vmem,) * 5,
        scratch_shapes=[
            buf(2, 8, 32, 8, 128),
            buf(2, 8, 32, 8, 128),
            buf(18, 32, 256),
            buf(18, 32, 256),
            buf(20, 32, 256),
            buf(2, 18, 256), buf(2, 18, 256), buf(2, 16, 256), buf(2, 16, 256),
            buf(2, 18, 256), buf(2, 18, 256), buf(2, 16, 256), buf(2, 16, 256),
            buf(8, 128), buf(8, 8, 128), buf(8, 8, 128),
            buf(8, 8, 128), buf(8, 8, 128), buf(4, 8, 128), buf(16, 8, 128),
            buf(4, 256, 256, dtype=BF16), buf(4, 256, 256, dtype=BF16),
            buf(4, 256, 256, dtype=BF16), buf(4, 256, 256, dtype=BF16),
            buf(256, 256), buf(256, 128),
            buf(256, 256, dtype=BF16), buf(256, 256, dtype=BF16),
            buf(256, 256, dtype=BF16), buf(256, 256, dtype=BF16),
            buf(256, 256, dtype=BF16), buf(256, 256, dtype=BF16),
            buf(256, 256), buf(256, 256), buf(4, 256, 256), buf(8, 128), buf(16, 256),
            buf(8, 32, 8, 128),
            buf(2, 4, 4, 8, 8, 128), buf(2, 4, 2, 4, 8, 128),
            buf(3, 8, 8, 128), buf(8, 3, 8, 8, 128),
            buf(8, 8, 128), buf(2, 4, 8, 128),
            pltpu.SemaphoreType.DMA((N_SLOTS,)),
            pltpu.SemaphoreType.DMA((N_SLOTS,)),
        ],
        compiler_params=pltpu.CompilerParams(
            collective_id=0, has_side_effects=True, vmem_limit_bytes=56 * 1024 * 1024
        ),
        name="block",
    )(state_field[0, 0], out_grad[0, 0], up_weight, down_weight, kg, seam_code[0])
    return (
        new[None, None],
        field[None, None],
        kgo[0, :36].reshape(9, 4),
        kgo[0, 36:40],
        up,
        down,
    )


def solution(mesh):
    placed = (
        P("face", "tile", None, None, None),
        P("face", "tile", None, None, None),
        P(None, "tile"),
        P("tile"),
        P("tile", None),
        P("tile", None),
        P("face", "tile", None),
    )
    return jax.shard_map(
        shards,
        mesh=mesh,
        in_specs=placed,
        out_specs=(
            P("face", "tile", None, None, None),
            P("face", "tile", None, None, None),
            P(None, "tile"),
            P("tile"),
            P("tile", None),
            P("tile", None),
        ),
        check_vma=False,
    )
```

time: 1830 us -> 92.7 us (0.05)
  blocking collectives: 1010 us -> 0 us
  waiting for transfers between devices: 746 us -> 0 us
  Pallas kernels: 0 us -> 83.9 us
  starting transfers between devices: 21.1 us -> 0 us
    unnamed x2 -> x0, blocking collectives: 566 us -> none
    reduce_scatter x1 -> x0, waiting for transfers between devices: 437 us -> none  [shards(): lax.psum_scatter(down_grad, 'tile', scatter_dimension=0, tiled=True)]
    all_gather x5 -> x0, blocking collectives: 368 us -> none  [the longest x1 200 us: shards(): lax.all_gather(depth_kernel, 'tile', axis=1, tiled=True)]
    unnamed x5 -> x0, waiting for transfers between devices: 309 us -> none
    pallas_call x0 -> x1, Pallas kernels: none -> 83.9 us  [shards(): pl.pallas_call(kernel, out_shape=(jax.ShapeDtypeStruct((16, 16, 256), F32...]
    psum x1 -> x0, blocking collectives: 76.1 us -> none  [shards(): lax.psum((shares[0], shares[1], shares[2], shares[3]), 'face')]
    ppermute x8 -> x0, starting transfers between devices: 20.7 us -> none  [shifted(): lax.ppermute(value, axis, [(source, source + steps) for source in range(i...]
  transfers between devices with their start and end apart: 12 -> 0, of which waited for: 2 -> 0; matrix products, arithmetic and copies ran while one was open for 1% -> 0% of each run, Pallas kernels for 0% -> 0%
where the time goes in v1:
time: 92.7 us; the launch traced here: 92.3 us
  Pallas kernels  83.9 us (91%)
  local copies, waits for them, and re-layouts  7.21 us (8%)
    pallas_call x1, Pallas kernels, shards(): pl.pallas_call(kernel, out_shape=(jax.ShapeDtypeStruct((16, 16, 256), F32...  83.9 us
    unnamed x18, local copies, waits for them, and re-layouts  6.44 us

profile of v1, /device:TPU:1, one launch (start us, length us, event | category | flops | bytes accessed | tf_op | source)
XLA Modules:
  0.0 92.3 jit_solution(17509162783036788674)
XLA Ops:
  0.6 0.0 copy-start.3
  0.6 0.7 copy-done.3
  1.3 0.1 copy.15
  1.4 0.1 reshape.18
  1.5 0.0 copy-start.4
  1.5 0.7 copy-done.4
  2.2 0.6 bitcast_maximum_fusion.kg
  2.7 83.9 %block.1 = (f32[16,16,256]{2,1,0:T(8,128)}, f32[16,16,256]{2,1,0:T(8,128)}, f32[4,1024]{1,0:T(4,128)}, f32[16,256]{1,0:T(8,128)}, f32[1,128]{1,0:T(1,128)}) custom-call(f32[16,16,256]{2,1,0:T(8,128)} %bitcast.10, f32[16,16,256]{2,1,0:T(8,128)} %bitcast.11, f32[4,1024]{1,0:T(4,128)} %up.1, f32[16,256]{1,0:T(8,128)} %down.1, f32[1,128]{1,0:T(1,128)} %bitcast_maximum_fusion.kg, ...), custom_call_target="tpu_custom_call" | custom-call | tf_op jit(solution)/shard_map/block/pallas_call | solution.py:721
  86.6 0.0 copy-start.5
  86.6 0.6 copy-done.5
  87.2 0.6 slice_bitcast_fusion
  87.8 0.1 reshape_squeeze.3
  87.9 0.7 copy.16
  88.6 0.0 copy-start
  88.6 1.7 %copy.21 = f32[1,1,16,16,256]{4,3,2,1,0:T(8,128)} copy(f32[1,1,16,16,256]{4,3,2,1,0:T(8,128)} %bitcast.13) | data formatting | bytes 524288
  90.3 0.0 copy-done
  90.3 0.0 copy-start.2
  90.3 0.7 copy.22
  91.0 0.0 copy-done.2
  91.0 0.0 copy-start.1
  91.0 0.6 copy.23
  91.6 0.1 copy-done.1
  91.7 0.6 copy.24
  (2 shorter events, 0.0 us)
Async XLA Ops:
  0.6 0.7 copy-start.3
  1.5 0.7 copy-start.4
  86.6 0.6 copy-start.5
  88.6 1.7 %copy-start = (f32[16,16,256]{2,1,0:T(8,128)S(1)}, f32[16,16,256]{2,1,0:T(8,128)}, u32[]{:S(2)}) copy-start(f32[16,16,256]{2,1,0:T(8,128)} %get-tuple-element.12) | copy-start | bytes 786436
  90.3 0.7 copy-start.2
  91.0 0.7 copy-start.1

commit v2 on v0

v2 whole, which is shorter than its diff:
```python
import functools
import math

import jax
import jax.numpy as jnp
from jax import lax
from jax.experimental import pallas as pl
from jax.experimental.pallas import tpu as pltpu
from jax.sharding import PartitionSpec as P

EPSILON = 1e-06
NX, NH, NY, NL, NC = 4, 2, 8, 4, 2
MESH = pl.DeviceIdType.MESH
F32, BF16 = jnp.float32, jnp.bfloat16
ROOT = math.sqrt(2.0 / math.pi)
NN = (((1,), (0,)), ((), ()))
NT = (((1,), (1,)), ((), ()))


class Slots:
    def __init__(self):
        self.used = 0

    def take(self, count):
        first = self.used
        self.used += count
        return first


SLOTS = Slots()
S_Y = SLOTS.take(8)
S_C = SLOTS.take(16)
S_X = SLOTS.take(48)
S_COT = SLOTS.take(1)
S_NORM = SLOTS.take(1)
S_KG1 = SLOTS.take(8)
S_KG2 = SLOTS.take(8)
S_HALO = SLOTS.take(4)
R_X = SLOTS.take(24)
R_Y = SLOTS.take(8)
R_Z = SLOTS.take(8)
R_F = SLOTS.take(2)
R_BR = SLOTS.take(2)
R_KY = SLOTS.take(8)
R_KX = SLOTS.take(4)
R_KZ = SLOTS.take(16)
R_HALO = SLOTS.take(4)
N_SLOTS = SLOTS.used

NEAR = (1, 7, 2, 6, 3, 5, 4)
FAR = (4, 3, 5, 2, 6, 1, 7, 0)


def split(value):
    high = value.astype(BF16)
    return high, (value - high.astype(F32)).astype(BF16)


def dot3(a, b, dims):
    def one(p, q):
        return lax.dot_general(p, q, dims, preferred_element_type=F32)

    return one(a[0], b[0]) + (one(a[0], b[1]) + one(a[1], b[0]))


def device(x, h, y, l, c):
    return (l * NC + c, (x * NH + h) * NY + y)


def kernel(
    state, cot, up, down, kt, gn, code,
    out_new, out_field, out_up, out_down, out_kg,
    w, g, west, middle, east, zpad, centre, wcol, ecol,
    ns_send, ns_recv, we_send, we_recv, bns_send, bns_recv, bwe_send, bwe_recv,
    kg_row, kg_own, kg_xh, kg_all, kgr_own, kgr_y, kgr_x, kgr_z,
    u_hi, u_lo, d_hi, d_lo, xhat, rstd, norm_own, norm_sib, cot_sib,
    n_hi, n_lo, nt_hi, nt_lo, g_hi, g_lo, branch, dnorm, br_recv, dn_recv, ugrad, dgrad, krows,
    x_recv, y_recv, z_recv, fin_up, fin_down,
    ssem, rsem,
):
    face, tile = lax.axis_index("face"), lax.axis_index("tile")
    l, c = face // 2, face % 2
    x, h, y = tile // 16, (tile // 8) % 2, tile % 8
    xh = x * 2 + h
    z = h * 4 + l
    same = (h + c) % 2
    ends = (l % 3 + 1) // 2

    def copy(src, dst, slot, to, send_slot=None):
        return pltpu.make_async_remote_copy(
            src_ref=src, dst_ref=dst,
            send_sem=ssem.at[slot if send_slot is None else send_slot], recv_sem=rsem.at[slot],
            device_id=to, device_id_type=MESH,
        )

    sibling = device(x, h, y, l, 1 - c)

    def arrived(dst, slot):
        copy(dst, dst, slot, sibling).wait_recv()

    def both(fn):
        pl.when(same == 0)(functools.partial(fn, True))
        pl.when(same == 1)(functools.partial(fn, False))

    barrier = pltpu.get_barrier_semaphore()
    peers = []
    for k in range(1, 16):
        peers.append(device(x, (h + k // 8) % 2, y, (l + (k // 2) % 4) % 4, (c + k % 2) % 2))
    for k in range(1, NY):
        peers.append(device(x, h, (y + k) % NY, l, c))
    for dx in range(1, NX):
        for dh in range(NH):
            peers.append(device((x + dx) % NX, (h + dh) % NH, y, l, c))
    mutual = len(peers)
    for k in range(NY):
        peers.append(device(x, 1 - h, (y + k) % NY, 3 * (1 - l // 2), c))
    for peer in peers:
        pl.semaphore_signal(barrier, inc=1, device_id=peer, device_id_type=MESH)

    def own_up(core, first):
        for e in range(2):
            low, high = (128 * (2 * (2 * e + bb) + core) for bb in range(2))
            w[y, x, first + e] = jnp.concatenate([up[:, low : low + 128], up[:, high : high + 128]], axis=0)

    def own_down():
        for rh in range(2):
            for q in range(2):
                w[y, x, 4 + 2 * rh + q] = down[8 * rh : 8 * rh + 8, 128 * q : 128 * q + 128]

    for core in range(2):
        for kind in range(2):

            def own(core=core, kind=kind):
                own_up(core, 2 if kind == 0 else 0)
                if kind == 0:
                    own_down()

            pl.when((c * 2 + same) == (core * 2 + kind))(own)

    sub8 = lax.broadcasted_iota(jnp.int32, (8, 128), 0)
    kg_row[...] = jnp.zeros_like(kg_row)
    for i in range(4):
        kg_row[i : i + 1, 0:9] = kt[i : i + 1, :]
        kg_row[i : i + 1, 9:10] = gn[0:1, i : i + 1]
    packed = kg_row[0:1, :]
    for i in range(1, 4):
        packed = packed + pltpu.roll(kg_row[i : i + 1, :], 32 * i, 1)
    kg_tile = jnp.where(sub8 == xh, jnp.broadcast_to(packed, (8, 128)), 0.0)
    kg_own[...] = kg_tile
    kg_xh[0] = kg_tile

    flips = [code[0, e].astype(F32) for e in range(4)]

    def mixed(flip, a, b):
        return a * (1.0 - flip) + b * flip

    for i in range(16):
        we_send[0, i : i + 1, :] = mixed(flips[2], state[i, 0:1, :], state[15 - i, 0:1, :])
        we_send[1, i : i + 1, :] = mixed(flips[3], state[i, 15:16, :], state[15 - i, 15:16, :])

    row, col = xh, y
    inner_n, inner_s = (row + 7) // 8, (14 - row) // 8
    inner_w, inner_e = (col + 7) // 8, (14 - col) // 8
    across = (
        (face + 4) % 8,
        7 - face,
        (face + 7 + 2 * (face % 2)) % 8,
        face + 1 - 2 * (face % 2),
    )

    def rim_copies(send, recv, base, stride, low_edge, high_edge, inner_low, inner_high):
        low_to = (
            inner_low * face + (1 - inner_low) * across[low_edge],
            tile - stride * inner_low,
        )
        high_to = (
            inner_high * face + (1 - inner_high) * across[high_edge],
            tile + stride * inner_high,
        )
        low = pltpu.make_async_remote_copy(
            src_ref=send.at[0], dst_ref=recv.at[inner_low], send_sem=ssem.at[base],
            recv_sem=rsem.at[base + inner_low], device_id=low_to, device_id_type=MESH,
        )
        high = pltpu.make_async_remote_copy(
            src_ref=send.at[1], dst_ref=recv.at[1 - inner_high], send_sem=ssem.at[base + 1],
            recv_sem=rsem.at[base + 1 - inner_high], device_id=high_to, device_id_type=MESH,
        )
        return low, high

    def prepare(r, carry):
        rows = state[pl.ds(r * 4, 4)]
        at = pl.ds(1 + r * 4, 4)
        middle[at] = rows
        west[at] = pltpu.roll(rows, 1, 1)
        east[at] = pltpu.roll(rows, 15, 1)
        high, low = split(cot[pl.ds(r * 4, 4)].reshape(64, 256))
        to = pl.ds(pl.multiple_of(r * 64, 64), 64)
        g_hi[0, to, :] = high
        g_lo[0, to, :] = low
        return carry

    lax.fori_loop(0, 4, prepare, 0)

    pl.semaphore_wait(barrier, mutual + 16 * (1 - ends))

    we = rim_copies(we_send, we_recv, S_HALO, 1, 2, 3, inner_w, inner_e)
    for each in we:
        each.start()

    def piece(yy, xx, whole):
        return w.at[yy, xx, 2:8] if whole else w.at[yy, xx, 0:2]

    def y_sends(whole):
        mine = piece(y, x, whole)
        return [copy(mine, mine, S_Y + k, device(x, h, (y + k) % NY, l, c)) for k in NEAR]

    def cross_sends(whole):
        mine = piece(y, x, whole)
        sends = []
        for k in (0, *NEAR):
            for m in range(2):
                ll = (3 - m) * (1 - l // 3) + m * (l // 3)
                to = device(x, 1 - h, (y + k) % NY, ll, c)
                sends.append(
                    pltpu.make_async_remote_copy(
                        src_ref=mine, dst_ref=mine, send_sem=ssem.at[S_C + 2 * k + m], recv_sem=rsem.at[S_C + k],
                        device_id=to, device_id_type=MESH,
                    )
                )
        return sends

    def x_sends(k, other, whole):
        ref = piece((y - k + NY) % NY, x, whole != other)
        return [
            copy(ref, ref, S_X + (2 * k + other) * 3 + dx - 1, device((x + dx) % NX, h, y, l, c))
            for dx in (2, 1, 3)
        ]

    def forward(k, other, whole):
        if k or other:
            arrived(piece((y - k + NY) % NY, x, whole != other), (S_C if other else S_Y) + k)
        for each in x_sends(k, other, whole):
            each.start()

    def first_leg(whole):
        for each in y_sends(whole):
            each.start()

        @pl.when(ends == 0)
        def _():
            for each in cross_sends(whole):
                each.start()

        forward(0, False, whole)

    both(first_leg)
    cot_copy = copy(cot, cot_sib, S_COT, sibling)
    cot_copy.start()
    kg1 = []
    for k in range(1, 8):
        dx, dh = k // 2, k % 2
        each = copy(kg_own, kg_xh.at[k], S_KG1 + k, device((x + dx) % NX, (h + dh) % NH, y, l, c))
        each.start()
        kg1.append(each)

    def second_leg(whole):
        forward(1, False, whole)
        forward(7, False, whole)

    both(second_leg)

    for k in range(2):
        arrived(we_recv.at[k], S_HALO + k)
    for i in range(16):
        west[1 + i, 0:1, :] = we_recv[0, i : i + 1, :]
        east[1 + i, 15:16, :] = we_recv[1, i : i + 1, :]
    for k, (edge, line) in enumerate(((0, 0), (1, 15))):
        first, last = we_recv[0, line : line + 1, :], we_recv[1, line : line + 1, :]
        ns_send[k, 0:1, :] = mixed(flips[edge], first, last)
        ns_send[k, 17:18, :] = mixed(flips[edge], last, first)
        for i in range(16):
            ns_send[k, 1 + i : 2 + i, :] = mixed(
                flips[edge], state[line, i : i + 1, :], state[line, 15 - i : 16 - i, :]
            )
    ns = rim_copies(ns_send, ns_recv, S_HALO + 2, 8, 0, 1, inner_n, inner_s)
    for each in ns:
        each.start()

    def third_leg(whole):
        for k, other in ((0, True), (2, False), (6, False), (1, True), (7, True), (3, False), (5, False)):
            forward(k, other, whole)

    both(third_leg)

    for k in range(1, 8):
        arrived(kg_xh.at[k], S_KG1 + k)
    total = kg_xh[0]
    for k in range(1, 8):
        total = total + kg_xh[k]
    kg_all[y] = total
    kg2 = []
    for k in range(1, NY):
        mine = kg_all.at[y]
        each = copy(mine, mine, S_KG2 + k, device(x, h, (y + k) % NY, l, c))
        each.start()
        kg2.append(each)

    def fourth_leg(whole):
        for k, other in ((2, True), (6, True), (4, False), (3, True), (5, True), (4, True)):
            forward(k, other, whole)

    both(fourth_leg)

    for k in range(1, NY):
        arrived(kg_all.at[(y - k + NY) % NY], S_KG2 + k)
    rows64 = lax.broadcasted_iota(jnp.int32, (64, 256), 0)
    chan = lax.broadcasted_iota(jnp.int32, (64, 256), 1)
    owner = (chan // 4) == ((rows64 % 8) * 8 + rows64 // 8)
    lane = lax.broadcasted_iota(jnp.int32, (64, 128), 1)
    same4 = (
        lax.broadcasted_iota(jnp.int32, (128, 256), 0) // 32
        == lax.broadcasted_iota(jnp.int32, (128, 256), 1) % 4
    )
    spread4 = jnp.where(same4, 1.0, 0.0).astype(BF16)
    tiles = kg_all[...].reshape(64, 128)
    grouped = jnp.concatenate([jnp.where(lane % 32 == k, tiles, 0.0) for k in range(10)], axis=0)
    first, second = split(grouped)
    spread_rows = lax.dot_general(first, spread4, NN, preferred_element_type=F32) + lax.dot_general(
        second, spread4, NN, preferred_element_type=F32
    )
    for k in range(10):
        krows[k : k + 1, :] = jnp.sum(
            jnp.where(owner, spread_rows[64 * k : 64 * k + 64], 0.0), axis=0, keepdims=True
        )

    for k in range(2):
        arrived(ns_recv.at[k], S_HALO + 2 + k)
        line = 17 * k
        west[line] = ns_recv[k, 0:16, :]
        middle[line] = ns_recv[k, 1:17, :]
        east[line] = ns_recv[k, 2:18, :]

    shifted = (west, middle, east)
    taps = [krows[k : k + 1, :] for k in range(9)]
    gain = krows[9:10, :]

    def conv_rows(r, carry):
        acc = jnp.zeros((4, 16, 256), F32)
        for i in range(3):
            for j in range(3):
                acc = acc + krows[3 * i + j : 3 * i + j + 1, :] * shifted[j][pl.ds(r * 4 + i, 4)]
        acc = acc.reshape(64, 256)
        mean = jnp.mean(acc, axis=-1, keepdims=True)
        centred = acc - mean
        var = jnp.mean(centred * centred, axis=-1, keepdims=True)
        inv = lax.rsqrt(var + EPSILON)
        hat = centred * inv
        at = pl.ds(pl.multiple_of(r * 64, 64), 64)
        xhat[at, :] = hat
        rstd[at, :] = jnp.broadcast_to(inv, (64, 128))
        normed = hat * krows[9:10, :]
        norm_own[at, :] = normed
        return carry

    lax.fori_loop(0, 4, conv_rows, 0)
    norm_copy = copy(norm_own, norm_sib, S_NORM, sibling)
    norm_copy.start()

    def prepare_tokens(m, source):
        def halves(r, carry):
            at = pl.ds(pl.multiple_of(r * 128, 128), 128)
            value = source[at, :]
            high, low = split(value)
            n_hi[m, at, :] = high
            n_lo[m, at, :] = low
            high, low = split(jnp.transpose(value))
            nt_hi[m, r] = high
            nt_lo[m, r] = low
            return carry

        lax.fori_loop(0, 2, halves, 0)

    prepare_tokens(0, norm_own)

    def x_arrivals(whole):
        for k in (0, *NEAR):
            for other in (False, True):
                for dx in (1, 3, 2):
                    ref = piece((y - k + NY) % NY, (x - dx + NX) % NX, whole != other)
                    arrived(ref, S_X + (2 * k + other) * 3 + dx - 1)

    both(x_arrivals)

    lows = lax.broadcasted_iota(jnp.int32, (4, 8, 128), 1) < 4

    def unpack(xs, carry):
        for r in range(2):
            hs = r * c + (1 - r) * (1 - c)
            at = pl.ds(pl.multiple_of(xs * 64 + hs * 32, 32), 32)
            for e in range(2):
                v = w[:, xs, 2 * r + e].reshape(4, 2, 8, 128)
                a, b = v[:, 0], v[:, 1]
                for bb, value in (
                    (0, jnp.where(lows, a, pltpu.roll(b, 4, 1))),
                    (1, jnp.where(lows, pltpu.roll(a, 4, 1), b)),
                ):
                    high, low = split(value.reshape(32, 128))
                    u_hi[e, at, 128 * bb : 128 * bb + 128] = high
                    u_lo[e, at, 128 * bb : 128 * bb + 128] = low
        at = pl.ds(pl.multiple_of((xs % 2) * 128, 128), 128)
        for q in range(2):
            value = jnp.concatenate([w[:, xs, 4 + q], w[:, xs, 6 + q]], axis=1).reshape(128, 128)
            high, low = split(value)
            d_hi[xs // 2, at, 128 * q : 128 * q + 128] = high
            d_lo[xs // 2, at, 128 * q : 128 * q + 128] = low
        return carry

    lax.fori_loop(0, NX, unpack, 0)

    arrived(cot_sib, S_COT)

    def prepare_cot(r, carry):
        high, low = split(cot_sib[pl.ds(r * 4, 4)].reshape(64, 256))
        to = pl.ds(pl.multiple_of(r * 64, 64), 64)
        g_hi[1, to, :] = high
        g_lo[1, to, :] = low
        return carry

    lax.fori_loop(0, 4, prepare_cot, 0)
    arrived(norm_sib, S_NORM)
    prepare_tokens(1, norm_sib)

    branch[...] = jnp.zeros_like(branch)
    dnorm[...] = jnp.zeros_like(dnorm)
    ugrad[...] = jnp.zeros_like(ugrad)
    dgrad[...] = jnp.zeros_like(dgrad)

    def chunk(step, carry):
        e, m = step // 2, step % 2
        normed = (n_hi[m], n_lo[m])
        grads = (g_hi[m], g_lo[m])
        ups = (u_hi[e], u_lo[e])
        downs = (d_hi[e], d_lo[e])
        pre = dot3(normed, ups, NN)
        back = dot3(grads, downs, NT)
        square = pre * pre
        t = jnp.tanh(ROOT * (pre + 0.044715 * (square * pre)))
        half = 0.5 * (1.0 + t)
        hidden = pre * half
        slope = half + 0.5 * pre * (1.0 - t * t) * (ROOT * (1.0 + 3 * 0.044715 * square))
        dpre = back * slope
        branch[m] += dot3(split(hidden), downs, NN)
        dp = split(dpre)
        dnorm[m] += dot3(dp, ups, NT)
        for r in range(2):
            part = tuple(v[128 * r : 128 * r + 128] for v in dp)
            ugrad[e] += dot3((nt_hi[m, r], nt_lo[m, r]), part, NN)
        dgrad[e] += dot3(split(jnp.transpose(hidden)), grads, NN)
        return carry

    lax.fori_loop(0, 4, chunk, 0)

    def pack(xs, carry):
        for r in range(2):
            hs = r * c + (1 - r) * (1 - c)
            at = pl.ds(pl.multiple_of(xs * 64 + hs * 32, 32), 32)
            for e in range(2):
                v0 = ugrad[e, at, 0:128].reshape(4, 8, 128)
                v1 = ugrad[e, at, 128:256].reshape(4, 8, 128)
                even = jnp.where(lows, v0, pltpu.roll(v1, 4, 1))
                odd = jnp.where(lows, pltpu.roll(v0, 4, 1), v1)
                g[:, xs, 2 * r + e] = jnp.concatenate([even[:, None], odd[:, None]], axis=1).reshape(8, 8, 128)
        at = pl.ds(pl.multiple_of((xs % 2) * 128, 128), 128)
        for q in range(2):
            v = dgrad[xs // 2, at, 128 * q : 128 * q + 128].reshape(8, 2, 8, 128)
            for rh in range(2):
                g[:, xs, 4 + 2 * rh + q] = v[:, rh]
        return carry

    lax.fori_loop(0, NX, pack, 0)

    swaps = [copy(dnorm.at[1], dn_recv, R_BR, sibling), copy(branch.at[1], br_recv, R_BR + 1, sibling)]
    swaps[0].start()
    reduces = []
    for k, offset in enumerate(FAR):
        yy = (y + offset) % NY
        for dx in (2, 1, 3):
            to = (x + dx) % NX
            each = copy(g.at[yy, to], x_recv.at[k, dx - 1], R_X + 3 * k + dx - 1, device(to, h, y, l, c))
            each.start()
            reduces.append(each)
    swaps[1].start()

    zpad[0:2] = jnp.zeros((2, 16, 256), F32)
    zpad[18:20] = jnp.zeros((2, 16, 256), F32)
    arrived(dn_recv, R_BR)

    def norm_rows(r, sums):
        at = pl.ds(pl.multiple_of(r * 32, 32), 32)
        hat = xhat[at, :]
        inv = rstd[at, :][:, 0:1]
        dn = dnorm[0, at, :] + dn_recv[at, :]
        dhat = dn * krows[9:10, :]
        mean = jnp.mean(dhat, axis=-1, keepdims=True)
        cross = jnp.mean(dhat * hat, axis=-1, keepdims=True)
        dd = (inv * (dhat - mean - hat * cross)).reshape(2, 16, 256)
        zpad[pl.ds(r * 2 + 2, 2)] = dd
        fresh = []
        for i in range(3):
            for j in range(3):
                v = (dd * shifted[j][pl.ds(r * 2 + i, 2)]).reshape(4, 8, 256)
                fresh.append(sums[3 * i + j] + ((v[0] + v[1]) + (v[2] + v[3])))
        v = (dn * hat).reshape(4, 8, 256)
        fresh.append(sums[9] + ((v[0] + v[1]) + (v[2] + v[3])))
        return tuple(fresh)

    sums = lax.fori_loop(0, 8, norm_rows, tuple(jnp.zeros((8, 256), F32) for _ in range(10)))

    lanes16 = lax.broadcasted_iota(jnp.int32, (2, 16, 256), 1)

    def back_rows(r, carry):
        parts = []
        for j in range(3):
            acc = jnp.zeros((2, 16, 256), F32)
            for i in range(3):
                acc = acc + krows[3 * i + j : 3 * i + j + 1, :] * zpad[pl.ds(r * 2 + 2 - i, 2)]
            parts.append(acc)
        to = pl.ds(r * 2, 2)
        left = jnp.where(lanes16 < 15, pltpu.roll(parts[0], 15, 1), 0.0)
        right = jnp.where(lanes16 > 0, pltpu.roll(parts[2], 1, 1), 0.0)
        centre[to] = parts[1] + (left + right)
        wcol[to] = parts[0][:, 0:1, :]
        ecol[to] = parts[2][:, 15:16, :]
        return carry

    lax.fori_loop(0, 9, back_rows, 0)
    for k, (edge, line) in enumerate(((0, 0), (1, 17))):
        first, last = wcol[line], ecol[line]
        bns_send[k, 0:1, :] = mixed(flips[edge], first, last)
        bns_send[k, 17:18, :] = mixed(flips[edge], last, first)
        for i in range(16):
            bns_send[k, 1 + i : 2 + i, :] = mixed(
                flips[edge], centre[line, i : i + 1, :], centre[line, 15 - i : 16 - i, :]
            )
    bns = rim_copies(bns_send, bns_recv, R_HALO, 8, 0, 1, inner_n, inner_s)
    for each in bns:
        each.start()

    grad_rows = [jnp.sum(sums[k], axis=0, keepdims=True) for k in range(10)]
    grouped = jnp.concatenate([jnp.where(owner, jnp.broadcast_to(v, (64, 256)), 0.0) for v in grad_rows], axis=0)
    first, second = split(grouped)
    fold = lax.dot_general(first, spread4, NT, preferred_element_type=F32) + lax.dot_general(
        second, spread4, NT, preferred_element_type=F32
    )
    folded = jnp.zeros((64, 128), F32)
    for k in range(10):
        folded = folded + jnp.where(lane % 32 == k, fold[64 * k : 64 * k + 64], 0.0)
    kgr_own[...] = folded.reshape(8, 8, 128)
    kgs = []
    for k in range(1, NY):
        yy = (y + k) % NY
        each = copy(kgr_own.at[yy], kgr_y.at[k], R_KY + k, device(x, h, yy, l, c))
        each.start()
        kgs.append(each)

    for k, offset in enumerate(FAR):
        yy = (y + offset) % NY
        for dx in (1, 3, 2):
            arrived(x_recv.at[k, dx - 1], R_X + 3 * k + dx - 1)
        g[yy, x] = (g[yy, x] + x_recv[k, 0]) + (x_recv[k, 1] + x_recv[k, 2])
        if offset:
            each = copy(g.at[yy, x], y_recv.at[offset], R_Y + offset, device(x, h, yy, l, c))
            each.start()
            reduces.append(each)

    arrived(br_recv, R_BR + 1)

    def new_rows(r, carry):
        at = pl.ds(pl.multiple_of(r * 64, 64), 64)
        value = branch[0, at, :] + br_recv[at, :]
        to = pl.ds(r * 4, 4)
        out_new[to] = state[to] + value.reshape(4, 16, 256)
        return carry

    lax.fori_loop(0, 4, new_rows, 0)

    for k, line in enumerate((1, 16)):
        arrived(bns_recv.at[k], R_HALO + k)
        wcol[line] = wcol[line] + bns_recv[k, 0:1, :]
        centre[line] = centre[line] + bns_recv[k, 1:17, :]
        ecol[line] = ecol[line] + bns_recv[k, 17:18, :]
    for i in range(16):
        bwe_send[0, i : i + 1, :] = mixed(flips[2], wcol[1 + i], wcol[16 - i])
        bwe_send[1, i : i + 1, :] = mixed(flips[3], ecol[1 + i], ecol[16 - i])
    bwe = rim_copies(bwe_send, bwe_recv, R_HALO + 2, 1, 2, 3, inner_w, inner_e)
    for each in bwe:
        each.start()

    for k in range(1, NY):
        arrived(kgr_y.at[k], R_KY + k)
    total = kgr_own[y]
    for k in range(1, NY):
        total = total + kgr_y[k]
    kgr_x[x] = total
    for k in range(1, NX):
        each = copy(kgr_x.at[x], kgr_x.at[x], R_KX + k, device((x + k) % NX, h, y, l, c))
        each.start()
        kgs.append(each)

    for k in range(1, NY):
        arrived(y_recv.at[k], R_Y + k)
    total = g[y, x]
    for k in range(1, NY):
        total = total + y_recv[k]
    z_recv[z] = total

    def z_sends(whole):
        sends = []
        for k in range(1, 8):
            dh, dl = k // 4, k % 4
            full = whole if dh == 0 else not whole
            ref = z_recv.at[z, 2:8] if full else z_recv.at[z, 0:2]
            sends.append(copy(ref, ref, R_Z + k, device(x, (h + dh) % NH, y, (l + dl) % NL, c)))
        return sends

    def z_start(whole):
        for each in z_sends(whole):
            each.start()

    both(z_start)

    for k in range(1, NX):
        arrived(kgr_x.at[(x - k + NX) % NX], R_KX + k)
    total = kgr_x[0]
    for k in range(1, NX):
        total = total + kgr_x[k]
    zc = z * 2 + c
    kgr_z[zc] = total
    for k in range(1, 16):
        to = device(x, (h + k // 8) % 2, y, (l + (k // 2) % 4) % 4, (c + k % 2) % 2)
        each = copy(kgr_z.at[zc], kgr_z.at[zc], R_KZ + k, to)
        each.start()
        kgs.append(each)

    for k in range(2):
        arrived(bwe_recv.at[k], R_HALO + 2 + k)
    for i in range(16):
        centre[1 + i, 0:1, :] = centre[1 + i, 0:1, :] + bwe_recv[0, i : i + 1, :]
        centre[1 + i, 15:16, :] = centre[1 + i, 15:16, :] + bwe_recv[1, i : i + 1, :]
        out_field[i] = centre[1 + i] + cot[i]

    def fin_sends(whole):
        sends = [copy(fin_up.at[c], fin_up.at[c], R_F, sibling)]
        if whole:
            sends.append(copy(fin_down, fin_down, R_F + 1, sibling))
        return sends

    def z_end(whole):
        for k in range(1, 8):
            zz = ((h + k // 4) % NH) * 4 + (l - k % 4 + NL) % NL
            arrived(z_recv.at[zz, 2:8] if whole else z_recv.at[zz, 0:2], R_Z + k)
        span = slice(2, 8) if whole else slice(0, 2)
        total = z_recv[0, span]
        for zz in range(1, 8):
            total = total + z_recv[zz, span]
        fin_up[c] = total[0:2]
        if whole:
            fin_down[...] = total[2:6]
        for each in fin_sends(whole):
            each.start()
        arrived(fin_up.at[1 - c], R_F)
        if not whole:
            arrived(fin_down, R_F + 1)

    both(z_end)
    for cc in range(2):
        for e in range(2):
            v = fin_up[cc, e]
            for bb in range(2):
                first = 128 * (2 * (2 * e + bb) + cc)
                out_up[:, first : first + 128] = v[4 * bb : 4 * bb + 4]
    for rh in range(2):
        for q in range(2):
            out_down[8 * rh : 8 * rh + 8, 128 * q : 128 * q + 128] = fin_down[2 * rh + q]

    for k in range(1, 16):
        hh, ll, cc = (h + k // 8) % 2, (l - (k // 2) % 4 + 4) % 4, (c + k % 2) % 2
        arrived(kgr_z.at[(hh * 4 + ll) * 2 + cc], R_KZ + k)
    total = kgr_z[0]
    for k in range(1, 16):
        total = total + kgr_z[k]
    out_kg[...] = jnp.sum(jnp.where(sub8 == xh, total, 0.0), axis=0, keepdims=True)

    def all_sent(whole):
        sends = y_sends(whole) + z_sends(whole) + fin_sends(whole)
        for k in range(NY):
            for other in (False, True):
                sends += x_sends(k, other, whole)
        for each in sends:
            each.wait_send()

        @pl.when(ends == 0)
        def _():
            for each in cross_sends(whole):
                each.wait_send()

    both(all_sent)
    for each in [*we, *kg1, *ns, *kg2, cot_copy, norm_copy, *swaps, *reduces, *bns, *kgs, *bwe]:
        each.wait_send()


def results(new, field, up, down, kg, out_new, out_field, out_up, out_down, out_kt, out_gn):
    out_new[...] = new[...]
    out_field[...] = field[...]
    out_up[...] = up[...]
    out_down[...] = down[...]
    for i in range(4):
        moved = kg[...] if i == 0 else pltpu.roll(kg[...], 128 - 32 * i, 1)
        out_kt[i : i + 1, :] = moved[:, 0:9]
        out_gn[0:1, i : i + 1] = moved[:, 9:10]


def shards(state_field, out_grad, depth_kernel, norm_gain, up_weight, down_weight, seam_code):
    vmem = pl.BlockSpec(memory_space=pltpu.VMEM)

    def buf(*shape, dtype=F32):
        return pltpu.VMEM(shape, dtype)

    def half(*shape):
        return pltpu.VMEM(shape, BF16)

    found = pl.pallas_call(
        kernel,
        out_shape=(
            jax.ShapeDtypeStruct((16, 16, 256), F32),
            jax.ShapeDtypeStruct((16, 16, 256), F32),
            jax.ShapeDtypeStruct((4, 1024), F32),
            jax.ShapeDtypeStruct((16, 256), F32),
            jax.ShapeDtypeStruct((1, 128), F32),
        ),
        in_specs=[vmem] * 6 + [pl.BlockSpec(memory_space=pltpu.SMEM)],
        out_specs=(vmem,) * 5,
        scratch_shapes=[
            buf(8, 4, 8, 8, 128), buf(8, 4, 8, 8, 128),
            buf(18, 16, 256), buf(18, 16, 256), buf(18, 16, 256),
            buf(20, 16, 256), buf(18, 16, 256), buf(18, 1, 256), buf(18, 1, 256),
            buf(2, 18, 256), buf(2, 18, 256), buf(2, 16, 256), buf(2, 16, 256),
            buf(2, 18, 256), buf(2, 18, 256), buf(2, 16, 256), buf(2, 16, 256),
            buf(8, 128), buf(8, 128), buf(8, 8, 128), buf(8, 8, 128),
            buf(8, 8, 128), buf(8, 8, 128), buf(4, 8, 128), buf(16, 8, 128),
            half(2, 256, 256), half(2, 256, 256), half(2, 256, 256), half(2, 256, 256),
            buf(256, 256), buf(256, 128), buf(256, 256), buf(256, 256), buf(16, 16, 256),
            half(2, 256, 256), half(2, 256, 256), half(2, 2, 256, 128), half(2, 2, 256, 128),
            half(2, 256, 256), half(2, 256, 256),
            buf(2, 256, 256), buf(2, 256, 256), buf(256, 256), buf(256, 256),
            buf(2, 256, 256), buf(2, 256, 256), buf(16, 256),
            buf(8, 3, 8, 8, 128), buf(8, 8, 8, 128), buf(8, 8, 8, 128),
            buf(2, 2, 8, 128), buf(4, 8, 128),
            pltpu.SemaphoreType.DMA((N_SLOTS,)),
            pltpu.SemaphoreType.DMA((N_SLOTS,)),
        ],
        compiler_params=pltpu.CompilerParams(
            collective_id=0, has_side_effects=True, vmem_limit_bytes=48 * 1024 * 1024
        ),
        name="block",
    )(
        state_field[0, 0], out_grad[0, 0], up_weight, down_weight,
        depth_kernel.T, norm_gain.reshape(1, 4), seam_code[0],
    )
    new, field, up, down, kt, gn = pl.pallas_call(
        results,
        out_shape=(
            jax.ShapeDtypeStruct((16, 16, 256), F32),
            jax.ShapeDtypeStruct((16, 16, 256), F32),
            jax.ShapeDtypeStruct((4, 1024), F32),
            jax.ShapeDtypeStruct((16, 256), F32),
            jax.ShapeDtypeStruct((4, 9), F32),
            jax.ShapeDtypeStruct((1, 4), F32),
        ),
        in_specs=[vmem] * 5,
        out_specs=(vmem,) * 6,
        name="results",
    )(*found)
    return (new[None, None], field[None, None], kt.T, gn.reshape(4), up, down)


def solution(mesh):
    placed = (
        P("face", "tile", None, None, None),
        P("face", "tile", None, None, None),
        P(None, "tile"),
        P("tile"),
        P("tile", None),
        P("tile", None),
        P("face", "tile", None),
    )
    return jax.shard_map(
        shards,
        mesh=mesh,
        in_specs=placed,
        out_specs=(
            P("face", "tile", None, None, None),
            P("face", "tile", None, None, None),
            P(None, "tile"),
            P("tile"),
            P("tile", None),
            P("tile", None),
        ),
        check_vma=False,
    )
```

time: 1830 us -> 76.1 us (0.04)
  blocking collectives: 1010 us -> 0 us
  waiting for transfers between devices: 746 us -> 0 us
  Pallas kernels: 0 us -> 68 us
  starting transfers between devices: 21.1 us -> 0 us
    unnamed x2 -> x0, blocking collectives: 566 us -> none
    reduce_scatter x1 -> x0, waiting for transfers between devices: 437 us -> none  [shards(): lax.psum_scatter(down_grad, 'tile', scatter_dimension=0, tiled=True)]
    all_gather x5 -> x0, blocking collectives: 368 us -> none  [the longest x1 200 us: shards(): lax.all_gather(depth_kernel, 'tile', axis=1, tiled=True)]
    unnamed x5 -> x0, waiting for transfers between devices: 309 us -> none
    psum x1 -> x0, blocking collectives: 76.1 us -> none  [shards(): lax.psum((shares[0], shares[1], shares[2], shares[3]), 'face')]
    pallas_call x0 -> x2, Pallas kernels: none -> 68 us  [the longest x1 66 us: shards(): pl.pallas_call(kernel, out_shape=(jax.ShapeDtypeStruct((16, 16, 256), F32...]
    ppermute x8 -> x0, starting transfers between devices: 20.7 us -> none  [shifted(): lax.ppermute(value, axis, [(source, source + steps) for source in range(i...]
  transfers between devices with their start and end apart: 12 -> 0, of which waited for: 2 -> 0; matrix products, arithmetic and copies ran while one was open for 1% -> 0% of each run, Pallas kernels for 0% -> 0%
where the time goes in v2:
time: 76.1 us; the launch traced here: 75.8 us
  Pallas kernels  68 us (89%)
  local copies, waits for them, and re-layouts  7.15 us (9%)
    pallas_call x1, Pallas kernels, shards(): pl.pallas_call(kernel, out_shape=(jax.ShapeDtypeStruct((16, 16, 256), F32...  66 us
    unnamed x24, local copies, waits for them, and re-layouts  7.15 us
    pallas_call x1, Pallas kernels, shards(): pl.pallas_call(results, out_shape=(jax.ShapeDtypeStruct((16, 16, 256), F3...  1.92 us

profile of v2, /device:TPU:1, one launch (start us, length us, event | category | flops | bytes accessed | tf_op | source)
XLA Modules:
  0.0 75.8 jit_solution(7256972757127769987)
XLA Ops:
  0.6 0.0 copy-start.8
  0.6 0.0 copy-start.10
  0.7 0.0 copy-start.11
  0.7 0.7 copy-done.8
  1.3 0.0 copy-done.10
  1.3 0.0 copy-done.11
  1.3 0.0 copy-start.2
  1.3 0.9 %copy-done.2 = f32[1,1,16,16,256]{4,3,2,1,0:T(8,128)S(1)} copy-done((f32[1,1,16,16,256]{4,3,2,1,0:T(8,128)S(1)}, f32[1,1,16,16,256]{4,3,2,1,0:T(8,128)}, u32[]{:S(2)}) %copy-start.2) | copy-done | bytes 262168
  2.3 0.0 copy-start.3
  2.3 0.9 %copy-done.3 = f32[1,1,16,16,256]{4,3,2,1,0:T(8,128)S(1)} copy-done((f32[1,1,16,16,256]{4,3,2,1,0:T(8,128)S(1)}, f32[1,1,16,16,256]{4,3,2,1,0:T(8,128)}, u32[]{:S(2)}) %copy-start.3) | copy-done | bytes 262168
  3.2 0.0 copy-start.4
  3.2 0.7 copy-done.4
  3.9 0.0 copy-start.5
  3.9 0.7 copy-done.5
  4.7 66.0 %block.1 = (f32[16,16,256]{2,1,0:T(8,128)S(1)}, f32[16,16,256]{2,1,0:T(8,128)S(1)}, f32[4,1024]{1,0:T(4,128)S(1)}, f32[16,256]{1,0:T(8,128)S(1)}, f32[1,128]{1,0:T(1,128)S(1)}) custom-call(f32[16,16,256]{2,1,0:T(8,128)S(1)} %bitcast.9, f32[16,16,256]{2,1,0:T(8,128)S(1)} %bitcast.10, f32[4,1024]{1,0:T(4,128)S(1)} %copy-done.4, f32[16,256]{1,0:T(8,128)S(1)} %copy-done.5, ...), custom_call_target="tpu_custom_call" | custom-call | tf_op jit(solution)/shard_map/block/pallas_call | solution.py:732
  70.7 0.0 copy-start
  70.7 0.7 copy-done
  71.4 0.0 copy-start.1
  71.4 0.7 copy-done.1
  72.1 0.0 copy-start.6
  72.1 0.6 copy-done.6
  72.7 0.6 copy-done.7
  73.3 0.6 copy-done.9
  73.9 1.9 %results.1 = (f32[16,16,256]{2,1,0:T(8,128)}, f32[16,16,256]{2,1,0:T(8,128)}, f32[4,1024]{1,0:T(4,128)}, f32[16,256]{1,0:T(8,128)}, f32[4,9]{1,0:T(4,128)}, /*index=5*/f32[1,4]{1,0:T(1,128)}) custom-call(f32[16,16,256]{2,1,0:T(8,128)} %copy-done, f32[16,16,256]{2,1,0:T(8,128)} %copy-done.1, f32[4,1024]{1,0:T(4,128)} %copy-done.6, f32[16,256]{1,0:T(8,128)} %copy-done.7, ...), custom_call_target="tpu_custom_call" | custom-call | tf_op jit(solution)/shard_map/results/pallas_call | solution.py:770
  (2 shorter events, 0.0 us)
Async XLA Ops:
  0.6 0.7 copy-start.8
  0.6 0.7 copy-start.10
  0.7 0.7 copy-start.11
  1.3 1.0 %copy-start.2 = (f32[1,1,16,16,256]{4,3,2,1,0:T(8,128)S(1)}, f32[1,1,16,16,256]{4,3,2,1,0:T(8,128)}, u32[]{:S(2)}) copy-start(f32[1,1,16,16,256]{4,3,2,1,0:T(8,128)} %param.7) | copy-start | bytes 786436
  2.3 0.9 %copy-start.3 = (f32[1,1,16,16,256]{4,3,2,1,0:T(8,128)S(1)}, f32[1,1,16,16,256]{4,3,2,1,0:T(8,128)}, u32[]{:S(2)}) copy-start(f32[1,1,16,16,256]{4,3,2,1,0:T(8,128)} %param.8) | copy-start | bytes 786436
  3.2 0.7 copy-start.4
  3.9 0.7 copy-start.5
  70.7 0.7 copy-start
  71.4 0.7 copy-start.1
  72.1 0.6 copy-start.6
  72.7 0.6 copy-start.7
  73.3 0.6 copy-start.9

commit v3 on v2

--- a/solution.py
+++ b/solution.py
@@ -30,13 +30,20 @@
 SLOTS = Slots()
 S_Y = SLOTS.take(8)
 S_C = SLOTS.take(16)
-S_X = SLOTS.take(48)
+S_X = SLOTS.take(24)
+S_BX = SLOTS.take(8)
+S_BY = SLOTS.take(8)
+S_IN = SLOTS.take(6)
+S_OUT = SLOTS.take(5)
 S_COT = SLOTS.take(1)
 S_NORM = SLOTS.take(1)
 S_KG1 = SLOTS.take(8)
 S_KG2 = SLOTS.take(8)
 S_HALO = SLOTS.take(4)
 R_X = SLOTS.take(24)
+R_XU = SLOTS.take(24)
+R_BY = SLOTS.take(8)
+R_BX = SLOTS.take(4)
 R_Y = SLOTS.take(8)
 R_Z = SLOTS.take(8)
 R_F = SLOTS.take(2)
@@ -68,14 +75,15 @@
 
 
 def kernel(
-    state, cot, up, down, kt, gn, code,
-    out_new, out_field, out_up, out_down, out_kg,
+    state_in, cot_in, up_in, down_in, kt_in, gn_in, code,
+    new_out, field_out, up_out, down_out, kg_out,
+    state, cot, up, down, kt, gn, out_new, out_field, out_up, out_down, out_kg,
     w, g, west, middle, east, zpad, centre, wcol, ecol,
     ns_send, ns_recv, we_send, we_recv, bns_send, bns_recv, bwe_send, bwe_recv,
     kg_row, kg_own, kg_xh, kg_all, kgr_own, kgr_y, kgr_x, kgr_z,
     u_hi, u_lo, d_hi, d_lo, xhat, rstd, norm_own, norm_sib, cot_sib,
-    n_hi, n_lo, nt_hi, nt_lo, g_hi, g_lo, branch, dnorm, br_recv, dn_recv, ugrad, dgrad, krows,
-    x_recv, y_recv, z_recv, fin_up, fin_down,
+    n_hi, n_lo, nt_hi, nt_lo, g_hi, g_lo, h_hi, h_lo, p_hi, p_lo, branch, dnorm, br_recv, dn_recv, ugrad, dgrad, krows,
+    x_recv, xu_recv, y_recv, by_recv, bx_recv, z_recv, fin_up, fin_down,
     ssem, rsem,
 ):
     face, tile = lax.axis_index("face"), lax.axis_index("tile")
@@ -111,11 +119,33 @@
     for dx in range(1, NX):
         for dh in range(NH):
             peers.append(device((x + dx) % NX, (h + dh) % NH, y, l, c))
-    mutual = len(peers)
-    for k in range(NY):
-        peers.append(device(x, 1 - h, (y + k) % NY, 3 * (1 - l // 2), c))
+    loads = [
+        pltpu.make_async_copy(src, dst, ssem.at[S_IN + k])
+        for k, (src, dst) in enumerate(
+            ((state_in, state), (kt_in, kt), (gn_in, gn), (up_in, up), (down_in, down), (cot_in, cot))
+        )
+    ]
+    for each in loads:
+        each.start()
+
+    def greet(peer):
+        pl.semaphore_signal(barrier, inc=1, device_id=peer, device_id_type=MESH)
+
     for peer in peers:
-        pl.semaphore_signal(barrier, inc=1, device_id=peer, device_id_type=MESH)
+        greet(peer)
+    source = 3 * (1 - l // 2)
+
+    def greet_sources(whole):
+        if whole:
+            for k in range(NX):
+                greet(device((x + k) % NX, 1 - h, y, source, c))
+        else:
+            for k in range(NY):
+                greet(device(x, 1 - h, (y + k) % NY, source, c))
+
+    both(greet_sources)
+    for each in loads:
+        each.wait()
 
     def own_up(core, first):
         for e in range(2):
@@ -201,49 +231,65 @@
 
     lax.fori_loop(0, 4, prepare, 0)
 
-    pl.semaphore_wait(barrier, mutual + 16 * (1 - ends))
+    pl.semaphore_wait(barrier, len(peers) + (1 - ends) * (16 - 8 * same))
 
     we = rim_copies(we_send, we_recv, S_HALO, 1, 2, 3, inner_w, inner_e)
     for each in we:
         each.start()
 
-    def piece(yy, xx, whole):
-        return w.at[yy, xx, 2:8] if whole else w.at[yy, xx, 0:2]
-
-    def y_sends(whole):
-        mine = piece(y, x, whole)
-        return [copy(mine, mine, S_Y + k, device(x, h, (y + k) % NY, l, c)) for k in NEAR]
+    def big(yy, xx):
+        return w.at[yy, xx, 2:8]
+
+    def small(yy, xx):
+        return w.at[yy, xx, 0:2]
+
+    def own_sends(whole):
+        mine = big(y, x) if whole else small(y, x)
+        if whole:
+            return [copy(mine, mine, S_Y + k, device(x, h, (y + k) % NY, l, c)) for k in NEAR]
+        return [copy(mine, mine, S_BX + k, device((x + k) % NX, h, y, l, c)) for k in (1, 3, 2)]
 
     def cross_sends(whole):
-        mine = piece(y, x, whole)
+        mine = big(y, x) if whole else small(y, x)
         sends = []
-        for k in (0, *NEAR):
+        for k in (0, *NEAR) if whole else (0, 1, 3, 2):
             for m in range(2):
                 ll = (3 - m) * (1 - l // 3) + m * (l // 3)
-                to = device(x, 1 - h, (y + k) % NY, ll, c)
+                if whole:
+                    to, slot = device(x, 1 - h, (y + k) % NY, ll, c), S_Y + k
+                else:
+                    to, slot = device((x + k) % NX, 1 - h, y, ll, c), S_BX + k
                 sends.append(
                     pltpu.make_async_remote_copy(
-                        src_ref=mine, dst_ref=mine, send_sem=ssem.at[S_C + 2 * k + m], recv_sem=rsem.at[S_C + k],
+                        src_ref=mine, dst_ref=mine, send_sem=ssem.at[S_C + 2 * k + m], recv_sem=rsem.at[slot],
                         device_id=to, device_id_type=MESH,
                     )
                 )
         return sends
 
-    def x_sends(k, other, whole):
-        ref = piece((y - k + NY) % NY, x, whole != other)
-        return [
-            copy(ref, ref, S_X + (2 * k + other) * 3 + dx - 1, device((x + dx) % NX, h, y, l, c))
-            for dx in (2, 1, 3)
-        ]
-
-    def forward(k, other, whole):
-        if k or other:
-            arrived(piece((y - k + NY) % NY, x, whole != other), (S_C if other else S_Y) + k)
-        for each in x_sends(k, other, whole):
+    def x_sends(k):
+        ref = big((y - k + NY) % NY, x)
+        return [copy(ref, ref, S_X + 3 * k + dx - 1, device((x + dx) % NX, h, y, l, c)) for dx in (2, 1, 3)]
+
+    def forward(k, whole):
+        if k or not whole:
+            arrived(big((y - k + NY) % NY, x), S_Y + k)
+        for each in x_sends(k):
             each.start()
 
+    def small_sends():
+        ref = w.at[y, :, 0:2]
+        return [copy(ref, ref, S_BY + k, device(x, h, (y + k) % NY, l, c)) for k in (4, 3, 5, 2, 6, 1, 7)]
+
+    def forward_small(whole):
+        for k in range(NX):
+            if k or whole:
+                arrived(small(y, (x - k + NX) % NX), S_BX + k)
+        for each in small_sends():
+            each.start()
+
     def first_leg(whole):
-        for each in y_sends(whole):
+        for each in own_sends(whole):
             each.start()
 
         @pl.when(ends == 0)
@@ -251,7 +297,8 @@
             for each in cross_sends(whole):
                 each.start()
 
-        forward(0, False, whole)
+        if whole:
+            forward(0, whole)
 
     both(first_leg)
     cot_copy = copy(cot, cot_sib, S_COT, sibling)
@@ -264,8 +311,11 @@
         kg1.append(each)
 
     def second_leg(whole):
-        forward(1, False, whole)
-        forward(7, False, whole)
+        if whole:
+            forward(1, whole)
+            forward(7, whole)
+        else:
+            forward(0, whole)
 
     both(second_leg)
 
@@ -287,8 +337,11 @@
         each.start()
 
     def third_leg(whole):
-        for k, other in ((0, True), (2, False), (6, False), (1, True), (7, True), (3, False), (5, False)):
-            forward(k, other, whole)
+        for k in (2, 6) if whole else (1, 7):
+            forward(k, whole)
+        forward_small(whole)
+        for k in (3, 5) if whole else (2, 6):
+            forward(k, whole)
 
     both(third_leg)
 
@@ -306,8 +359,8 @@
         kg2.append(each)
 
     def fourth_leg(whole):
-        for k, other in ((2, True), (6, True), (4, False), (3, True), (5, True), (4, True)):
-            forward(k, other, whole)
+        for k in (4,) if whole else (3, 5, 4):
+            forward(k, whole)
 
     both(fourth_leg)
 
@@ -382,14 +435,11 @@
 
     prepare_tokens(0, norm_own)
 
-    def x_arrivals(whole):
-        for k in (0, *NEAR):
-            for other in (False, True):
-                for dx in (1, 3, 2):
-                    ref = piece((y - k + NY) % NY, (x - dx + NX) % NX, whole != other)
-                    arrived(ref, S_X + (2 * k + other) * 3 + dx - 1)
-
-    both(x_arrivals)
+    for k in NEAR:
+        arrived(w.at[(y - k + NY) % NY, :, 0:2], S_BY + k)
+    for k in (0, *NEAR):
+        for dx in (1, 3, 2):
+            arrived(big((y - k + NY) % NY, (x - dx + NX) % NX), S_X + 3 * k + dx - 1)
 
     lows = lax.broadcasted_iota(jnp.int32, (4, 8, 128), 1) < 4
 
@@ -430,35 +480,55 @@
     arrived(norm_sib, S_NORM)
     prepare_tokens(1, norm_sib)
 
-    branch[...] = jnp.zeros_like(branch)
-    dnorm[...] = jnp.zeros_like(dnorm)
-    ugrad[...] = jnp.zeros_like(ugrad)
-    dgrad[...] = jnp.zeros_like(dgrad)
-
-    def chunk(step, carry):
-        e, m = step // 2, step % 2
-        normed = (n_hi[m], n_lo[m])
-        grads = (g_hi[m], g_lo[m])
+    def first_products(e, carry):
+        downs = (d_hi[e], d_lo[e])
         ups = (u_hi[e], u_lo[e])
-        downs = (d_hi[e], d_lo[e])
-        pre = dot3(normed, ups, NN)
-        back = dot3(grads, downs, NT)
-        square = pre * pre
-        t = jnp.tanh(ROOT * (pre + 0.044715 * (square * pre)))
-        half = 0.5 * (1.0 + t)
-        hidden = pre * half
-        slope = half + 0.5 * pre * (1.0 - t * t) * (ROOT * (1.0 + 3 * 0.044715 * square))
-        dpre = back * slope
-        branch[m] += dot3(split(hidden), downs, NN)
-        dp = split(dpre)
-        dnorm[m] += dot3(dp, ups, NT)
-        for r in range(2):
-            part = tuple(v[128 * r : 128 * r + 128] for v in dp)
-            ugrad[e] += dot3((nt_hi[m, r], nt_lo[m, r]), part, NN)
-        dgrad[e] += dot3(split(jnp.transpose(hidden)), grads, NN)
+        total = jnp.zeros((256, 256), F32)
+        for m in range(2):
+            grads = (g_hi[m], g_lo[m])
+            pre = dot3((n_hi[m], n_lo[m]), ups, NN)
+            back = dot3(grads, downs, NT)
+            square = pre * pre
+            t = jnp.tanh(ROOT * (pre + 0.044715 * (square * pre)))
+            half = 0.5 * (1.0 + t)
+            hidden = pre * half
+            slope = half + 0.5 * pre * (1.0 - t * t) * (ROOT * (1.0 + 3 * 0.044715 * square))
+            high, low = split(back * slope)
+            p_hi[m, e] = high
+            p_lo[m, e] = low
+            high, low = split(hidden)
+            h_hi[m, e] = high
+            h_lo[m, e] = low
+            total = total + dot3(split(jnp.transpose(hidden)), grads, NN)
+        for bb in range(2):
+            for q in range(2):
+                v = total[128 * bb : 128 * bb + 128, 128 * q : 128 * q + 128].reshape(8, 2, 8, 128)
+                for rh in range(2):
+                    g[:, 2 * e + bb, 4 + 2 * rh + q] = v[:, rh]
         return carry
 
-    lax.fori_loop(0, 4, chunk, 0)
+    lax.fori_loop(0, 2, first_products, 0)
+
+    reduces = []
+    for k, offset in enumerate(FAR):
+        yy = (y + offset) % NY
+        for dx in (2, 1, 3):
+            to = (x + dx) % NX
+            each = copy(
+                g.at[yy, to, 4:8], x_recv.at[k, dx - 1], R_X + 3 * k + dx - 1, device(to, h, y, l, c)
+            )
+            each.start()
+            reduces.append(each)
+
+    def second_products(e, carry):
+        ugrad[e] = sum(
+            dot3((nt_hi[m, r], nt_lo[m, r]), (p_hi[m, e, 128 * r : 128 * r + 128], p_lo[m, e, 128 * r : 128 * r + 128]), NN)
+            for m in range(2)
+            for r in range(2)
+        )
+        return carry
+
+    lax.fori_loop(0, 2, second_products, 0)
 
     def pack(xs, carry):
         for r in range(2):
@@ -470,26 +540,33 @@
                 even = jnp.where(lows, v0, pltpu.roll(v1, 4, 1))
                 odd = jnp.where(lows, pltpu.roll(v0, 4, 1), v1)
                 g[:, xs, 2 * r + e] = jnp.concatenate([even[:, None], odd[:, None]], axis=1).reshape(8, 8, 128)
-        at = pl.ds(pl.multiple_of((xs % 2) * 128, 128), 128)
-        for q in range(2):
-            v = dgrad[xs // 2, at, 128 * q : 128 * q + 128].reshape(8, 2, 8, 128)
-            for rh in range(2):
-                g[:, xs, 4 + 2 * rh + q] = v[:, rh]
         return carry
 
     lax.fori_loop(0, NX, pack, 0)
-
-    swaps = [copy(dnorm.at[1], dn_recv, R_BR, sibling), copy(branch.at[1], br_recv, R_BR + 1, sibling)]
-    swaps[0].start()
-    reduces = []
+    for k in (4, 3, 5, 2, 6, 1, 7):
+        yy = (y + k) % NY
+        each = copy(g.at[yy, :, 0:2], by_recv.at[k], R_BY + k, device(x, h, yy, l, c))
+        each.start()
+        reduces.append(each)
     for k, offset in enumerate(FAR):
         yy = (y + offset) % NY
         for dx in (2, 1, 3):
             to = (x + dx) % NX
-            each = copy(g.at[yy, to], x_recv.at[k, dx - 1], R_X + 3 * k + dx - 1, device(to, h, y, l, c))
+            each = copy(
+                g.at[yy, to, 2:4], xu_recv.at[k, dx - 1], R_XU + 3 * k + dx - 1, device(to, h, y, l, c)
+            )
             each.start()
             reduces.append(each)
-    swaps[1].start()
+
+    swaps = [copy(dnorm.at[1], dn_recv, R_BR, sibling), copy(branch.at[1], br_recv, R_BR + 1, sibling)]
+    for m in (1, 0):
+        dnorm[m] = sum(dot3((p_hi[m, e], p_lo[m, e]), (u_hi[e], u_lo[e]), NT) for e in range(2))
+        if m:
+            swaps[0].start()
+    for m in (1, 0):
+        branch[m] = sum(dot3((h_hi[m, e], h_lo[m, e]), (d_hi[e], d_lo[e]), NN) for e in range(2))
+        if m:
+            swaps[1].start()
 
     zpad[0:2] = jnp.zeros((2, 16, 256), F32)
     zpad[18:20] = jnp.zeros((2, 16, 256), F32)
@@ -563,13 +640,27 @@
         each.start()
         kgs.append(each)
 
+    for k in range(1, NY):
+        arrived(by_recv.at[k], R_BY + k)
+    total = g[y, :, 0:2]
+    for k in range(1, NY):
+        total = total + by_recv[k]
+    g[y, :, 0:2] = total
+    for dx in (2, 1, 3):
+        to = (x + dx) % NX
+        each = copy(g.at[y, to, 0:2], bx_recv.at[dx], R_BX + dx, device(to, h, y, l, c))
+        each.start()
+        reduces.append(each)
+
     for k, offset in enumerate(FAR):
         yy = (y + offset) % NY
         for dx in (1, 3, 2):
             arrived(x_recv.at[k, dx - 1], R_X + 3 * k + dx - 1)
-        g[yy, x] = (g[yy, x] + x_recv[k, 0]) + (x_recv[k, 1] + x_recv[k, 2])
+            arrived(xu_recv.at[k, dx - 1], R_XU + 3 * k + dx - 1)
+        g[yy, x, 4:8] = (g[yy, x, 4:8] + x_recv[k, 0]) + (x_recv[k, 1] + x_recv[k, 2])
+        g[yy, x, 2:4] = (g[yy, x, 2:4] + xu_recv[k, 0]) + (xu_recv[k, 1] + xu_recv[k, 2])
         if offset:
-            each = copy(g.at[yy, x], y_recv.at[offset], R_Y + offset, device(x, h, yy, l, c))
+            each = copy(g.at[yy, x, 2:8], y_recv.at[offset], R_Y + offset, device(x, h, yy, l, c))
             each.start()
             reduces.append(each)
 
@@ -583,6 +674,8 @@
         return carry
 
     lax.fori_loop(0, 4, new_rows, 0)
+    stores = [pltpu.make_async_copy(out_new, new_out, rsem.at[S_OUT])]
+    stores[0].start()
 
     for k, line in enumerate((1, 16)):
         arrived(bns_recv.at[k], R_HALO + k)
@@ -609,10 +702,13 @@
 
     for k in range(1, NY):
         arrived(y_recv.at[k], R_Y + k)
-    total = g[y, x]
+    total = g[y, x, 2:8]
     for k in range(1, NY):
         total = total + y_recv[k]
-    z_recv[z] = total
+    z_recv[z, 2:8] = total
+    for dx in range(1, NX):
+        arrived(bx_recv.at[dx], R_BX + dx)
+    z_recv[z, 0:2] = (g[y, x, 0:2] + bx_recv[1]) + (bx_recv[2] + bx_recv[3])
 
     def z_sends(whole):
         sends = []
@@ -648,6 +744,8 @@
         centre[1 + i, 0:1, :] = centre[1 + i, 0:1, :] + bwe_recv[0, i : i + 1, :]
         centre[1 + i, 15:16, :] = centre[1 + i, 15:16, :] + bwe_recv[1, i : i + 1, :]
         out_field[i] = centre[1 + i] + cot[i]
+    stores.append(pltpu.make_async_copy(out_field, field_out, rsem.at[S_OUT + 1]))
+    stores[1].start()
 
     def fin_sends(whole):
         sends = [copy(fin_up.at[c], fin_up.at[c], R_F, sibling)]
@@ -682,6 +780,10 @@
     for rh in range(2):
         for q in range(2):
             out_down[8 * rh : 8 * rh + 8, 128 * q : 128 * q + 128] = fin_down[2 * rh + q]
+    stores.append(pltpu.make_async_copy(out_up, up_out, rsem.at[S_OUT + 2]))
+    stores.append(pltpu.make_async_copy(out_down, down_out, rsem.at[S_OUT + 3]))
+    stores[2].start()
+    stores[3].start()
 
     for k in range(1, 16):
         hh, ll, cc = (h + k // 8) % 2, (l - (k // 2) % 4 + 4) % 4, (c + k % 2) % 2
@@ -690,13 +792,11 @@
     for k in range(1, 16):
         total = total + kgr_z[k]
     out_kg[...] = jnp.sum(jnp.where(sub8 == xh, total, 0.0), axis=0, keepdims=True)
+    stores.append(pltpu.make_async_copy(out_kg, kg_out, rsem.at[S_OUT + 4]))
+    stores[4].start()
 
     def all_sent(whole):
-        sends = y_sends(whole) + z_sends(whole) + fin_sends(whole)
-        for k in range(NY):
-            for other in (False, True):
-                sends += x_sends(k, other, whole)
-        for each in sends:
+        for each in own_sends(whole) + z_sends(whole) + fin_sends(whole):
             each.wait_send()
 
         @pl.when(ends == 0)
@@ -705,23 +805,47 @@
                 each.wait_send()
 
     both(all_sent)
-    for each in [*we, *kg1, *ns, *kg2, cot_copy, norm_copy, *swaps, *reduces, *bns, *kgs, *bwe]:
+    for k in range(NY):
+        for each in x_sends(k):
+            each.wait_send()
+    for each in [
+        *small_sends(), *we, *kg1, *ns, *kg2, cot_copy, norm_copy, *swaps, *reduces, *bns, *kgs, *bwe
+    ]:
         each.wait_send()
-
-
-def results(new, field, up, down, kg, out_new, out_field, out_up, out_down, out_kt, out_gn):
-    out_new[...] = new[...]
-    out_field[...] = field[...]
-    out_up[...] = up[...]
-    out_down[...] = down[...]
+    for each in stores:
+        each.wait()
+
+
+def results(
+    new, field, up, down, kg, out_new, out_field, out_up, out_down, out_kt, out_gn,
+    v_new, v_field, v_up, v_down, v_kg, v_kt, v_gn, sem,
+):
+    held = (v_kg, v_new, v_field, v_up, v_down)
+    reads = [pltpu.make_async_copy(src, dst, sem.at[k]) for k, (src, dst) in enumerate(zip((kg, new, field, up, down), held))]
+    writes = [
+        pltpu.make_async_copy(src, dst, sem.at[5 + k])
+        for k, (src, dst) in enumerate(
+            ((v_new, out_new), (v_field, out_field), (v_up, out_up), (v_down, out_down), (v_kt, out_kt), (v_gn, out_gn))
+        )
+    ]
+    for each in reads:
+        each.start()
+    reads[0].wait()
     for i in range(4):
-        moved = kg[...] if i == 0 else pltpu.roll(kg[...], 128 - 32 * i, 1)
-        out_kt[i : i + 1, :] = moved[:, 0:9]
-        out_gn[0:1, i : i + 1] = moved[:, 9:10]
+        moved = v_kg[...] if i == 0 else pltpu.roll(v_kg[...], 128 - 32 * i, 1)
+        v_kt[i : i + 1, :] = moved[:, 0:9]
+        v_gn[0:1, i : i + 1] = moved[:, 9:10]
+    writes[4].start()
+    writes[5].start()
+    for k in range(4):
+        reads[1 + k].wait()
+        writes[k].start()
+    for each in writes:
+        each.wait()
 
 
 def shards(state_field, out_grad, depth_kernel, norm_gain, up_weight, down_weight, seam_code):
-    vmem = pl.BlockSpec(memory_space=pltpu.VMEM)
+    anywhere = pl.BlockSpec(memory_space=pl.ANY)
 
     def buf(*shape, dtype=F32):
         return pltpu.VMEM(shape, dtype)
@@ -738,9 +862,11 @@
             jax.ShapeDtypeStruct((16, 256), F32),
             jax.ShapeDtypeStruct((1, 128), F32),
         ),
-        in_specs=[vmem] * 6 + [pl.BlockSpec(memory_space=pltpu.SMEM)],
-        out_specs=(vmem,) * 5,
+        in_specs=[anywhere] * 6 + [pl.BlockSpec(memory_space=pltpu.SMEM)],
+        out_specs=(anywhere,) * 5,
         scratch_shapes=[
+            buf(16, 16, 256), buf(16, 16, 256), buf(4, 1024), buf(16, 256), buf(4, 9), buf(1, 4),
+            buf(16, 16, 256), buf(16, 16, 256), buf(4, 1024), buf(16, 256), buf(1, 128),
             buf(8, 4, 8, 8, 128), buf(8, 4, 8, 8, 128),
             buf(18, 16, 256), buf(18, 16, 256), buf(18, 16, 256),
             buf(20, 16, 256), buf(18, 16, 256), buf(18, 1, 256), buf(18, 1, 256),
@@ -752,15 +878,17 @@
             buf(256, 256), buf(256, 128), buf(256, 256), buf(256, 256), buf(16, 16, 256),
             half(2, 256, 256), half(2, 256, 256), half(2, 2, 256, 128), half(2, 2, 256, 128),
             half(2, 256, 256), half(2, 256, 256),
+            half(2, 2, 256, 256), half(2, 2, 256, 256), half(2, 2, 256, 256), half(2, 2, 256, 256),
             buf(2, 256, 256), buf(2, 256, 256), buf(256, 256), buf(256, 256),
             buf(2, 256, 256), buf(2, 256, 256), buf(16, 256),
-            buf(8, 3, 8, 8, 128), buf(8, 8, 8, 128), buf(8, 8, 8, 128),
+            buf(8, 3, 4, 8, 128), buf(8, 3, 2, 8, 128), buf(8, 6, 8, 128),
+            buf(8, 4, 2, 8, 128), buf(4, 2, 8, 128), buf(8, 8, 8, 128),
             buf(2, 2, 8, 128), buf(4, 8, 128),
             pltpu.SemaphoreType.DMA((N_SLOTS,)),
             pltpu.SemaphoreType.DMA((N_SLOTS,)),
         ],
         compiler_params=pltpu.CompilerParams(
-            collective_id=0, has_side_effects=True, vmem_limit_bytes=48 * 1024 * 1024
+            collective_id=0, has_side_effects=True, vmem_limit_bytes=60 * 1024 * 1024
         ),
         name="block",
     )(
@@ -777,8 +905,13 @@
             jax.ShapeDtypeStruct((4, 9), F32),
             jax.ShapeDtypeStruct((1, 4), F32),
         ),
-        in_specs=[vmem] * 5,
-        out_specs=(vmem,) * 6,
+        in_specs=[anywhere] * 5,
+        out_specs=(anywhere,) * 6,
+        scratch_shapes=[
+            buf(16, 16, 256), buf(16, 16, 256), buf(4, 1024), buf(16, 256), buf(1, 128), buf(4, 9), buf(1, 4),
+            pltpu.SemaphoreType.DMA((11,)),
+        ],
+        compiler_params=pltpu.CompilerParams(vmem_limit_bytes=60 * 1024 * 1024),
         name="results",
     )(*found)
     return (new[None, None], field[None, None], kt.T, gn.reshape(4), up, down)

time: 76.1 us -> 69.9 us (0.919)
  local copies, waits for them, and re-layouts: 7.15 us -> 0 us
  Pallas kernels: 68 us -> 69.1 us
    unnamed x24 -> x0, local copies, waits for them, and re-layouts: 7.15 us -> none
    pallas_call x1, Pallas kernels: 66 us -> 67.2 us  [shards(): pl.pallas_call(kernel, out_shape=(jax.ShapeDtypeStruct((16, 16, 256), F32...]
where the time goes in v3:
time: 69.9 us; the launch traced here: 69.7 us
  Pallas kernels  69.1 us (99%)
    pallas_call x1, Pallas kernels, shards(): pl.pallas_call(kernel, out_shape=(jax.ShapeDtypeStruct((16, 16, 256), F32...  67.2 us
    pallas_call x1, Pallas kernels, shards(): pl.pallas_call(results, out_shape=(jax.ShapeDtypeStruct((16, 16, 256), F3...  1.85 us

profile of v3, /device:TPU:1, one launch (start us, length us, event | category | flops | bytes accessed | tf_op | source)
XLA Modules:
  0.0 69.7 jit_solution(4357974009548541148)
XLA Ops:
  0.6 67.2 %block.1 = (f32[16,16,256]{2,1,0:T(8,128)}, f32[16,16,256]{2,1,0:T(8,128)}, f32[4,1024]{1,0:T(4,128)}, f32[16,256]{1,0:T(8,128)}, f32[1,128]{1,0:T(1,128)}) custom-call(f32[16,16,256]{2,1,0:T(8,128)} %bitcast.9, f32[16,16,256]{2,1,0:T(8,128)} %bitcast.10, f32[4,1024]{1,0:T(4,128)} %up_in.1, f32[16,256]{1,0:T(8,128)} %down_in.1, f32[4,9]{1,0:T(4,128)} %bitcast.11, ...), custom_call_target="tpu_custom_call" | custom-call | tf_op jit(solution)/shard_map/block/pallas_call | solution.py:856
  67.9 1.8 %results.1 = (f32[16,16,256]{2,1,0:T(8,128)}, f32[16,16,256]{2,1,0:T(8,128)}, f32[4,1024]{1,0:T(4,128)}, f32[16,256]{1,0:T(8,128)}, f32[4,9]{1,0:T(4,128)}, /*index=5*/f32[1,4]{1,0:T(1,128)}) custom-call(f32[16,16,256]{2,1,0:T(8,128)} %get-tuple-element.17.new, f32[16,16,256]{2,1,0:T(8,128)} %get-tuple-element.18.field, f32[4,1024]{1,0:T(4,128)} %get-tuple-element.19.up, ...), custom_call_target="tpu_custom_call" | custom-call | tf_op jit(solution)/shard_map/results/pallas_call | solution.py:898

commit v4 on v3

--- a/solution.py
+++ b/solution.py
@@ -36,12 +36,12 @@
 S_IN = SLOTS.take(6)
 S_OUT = SLOTS.take(5)
 S_COT = SLOTS.take(1)
-S_NORM = SLOTS.take(1)
+S_NORM = SLOTS.take(4)
 S_KG1 = SLOTS.take(8)
 S_KG2 = SLOTS.take(8)
 S_HALO = SLOTS.take(4)
-R_X = SLOTS.take(24)
-R_XU = SLOTS.take(24)
+R_X = SLOTS.take(6)
+R_XU = SLOTS.take(6)
 R_BY = SLOTS.take(8)
 R_BX = SLOTS.take(4)
 R_Y = SLOTS.take(8)
@@ -55,7 +55,6 @@
 N_SLOTS = SLOTS.used
 
 NEAR = (1, 7, 2, 6, 3, 5, 4)
-FAR = (4, 3, 5, 2, 6, 1, 7, 0)
 
 
 def split(value):
@@ -68,10 +67,6 @@
         return lax.dot_general(p, q, dims, preferred_element_type=F32)
 
     return one(a[0], b[0]) + (one(a[0], b[1]) + one(a[1], b[0]))
-
-
-def device(x, h, y, l, c):
-    return (l * NC + c, (x * NH + h) * NY + y)
 
 
 def kernel(
@@ -89,6 +84,35 @@
     face, tile = lax.axis_index("face"), lax.axis_index("tile")
     l, c = face // 2, face % 2
     x, h, y = tile // 16, (tile // 8) % 2, tile % 8
+    xs_at = [x] + [(x + k) % NX for k in range(1, NX)]
+    ys_at = [y] + [(y + k) % NY for k in range(1, NY)]
+    hs_at = [h, 1 - h]
+    ls_at = [l] + [(l + k) % NL for k in range(1, NL)]
+    cs_at = [c, 1 - c]
+    cross_l = [(3 - m) * (1 - l // 3) + m * (l // 3) for m in range(2)]
+    source = 3 * (1 - l // 2)
+    known = {}
+
+    def device(x, h, y, l, c):
+        key = (id(x), id(h), id(y), id(l), id(c))
+        return known[key] if key in known else (l * NC + c, (x * NH + h) * NY + y)
+
+    def remember(*place):
+        known[tuple(id(v) for v in place)] = device(*place)
+
+    for k in range(NY):
+        remember(x, h, ys_at[k], l, c)
+        for ll in (*cross_l, source):
+            remember(x, hs_at[1], ys_at[k], ll, c)
+    for k in range(NX):
+        for hh in hs_at:
+            remember(xs_at[k], hh, y, l, c)
+        for ll in (*cross_l, source):
+            remember(xs_at[k], hs_at[1], y, ll, c)
+    for hh in hs_at:
+        for ll in ls_at:
+            for cc in cs_at:
+                remember(x, hh, y, ll, cc)
     xh = x * 2 + h
     z = h * 4 + l
     same = (h + c) % 2
@@ -101,7 +125,7 @@
             device_id=to, device_id_type=MESH,
         )
 
-    sibling = device(x, h, y, l, 1 - c)
+    sibling = device(x, h, y, l, cs_at[1])
 
     def arrived(dst, slot):
         copy(dst, dst, slot, sibling).wait_recv()
@@ -113,12 +137,12 @@
     barrier = pltpu.get_barrier_semaphore()
     peers = []
     for k in range(1, 16):
-        peers.append(device(x, (h + k // 8) % 2, y, (l + (k // 2) % 4) % 4, (c + k % 2) % 2))
-    for k in range(1, NY):
-        peers.append(device(x, h, (y + k) % NY, l, c))
+        peers.append(device(x, hs_at[k // 8], y, ls_at[(k // 2) % 4], cs_at[k % 2]))
+    for k in range(1, NY):
+        peers.append(device(x, h, ys_at[k], l, c))
     for dx in range(1, NX):
         for dh in range(NH):
-            peers.append(device((x + dx) % NX, (h + dh) % NH, y, l, c))
+            peers.append(device(xs_at[dx], hs_at[dh], y, l, c))
     loads = [
         pltpu.make_async_copy(src, dst, ssem.at[S_IN + k])
         for k, (src, dst) in enumerate(
@@ -133,15 +157,13 @@
 
     for peer in peers:
         greet(peer)
-    source = 3 * (1 - l // 2)
-
     def greet_sources(whole):
         if whole:
             for k in range(NX):
-                greet(device((x + k) % NX, 1 - h, y, source, c))
+                greet(device(xs_at[k], hs_at[1], y, source, c))
         else:
             for k in range(NY):
-                greet(device(x, 1 - h, (y + k) % NY, source, c))
+                greet(device(x, hs_at[1], ys_at[k], source, c))
 
     both(greet_sources)
     for each in loads:
@@ -246,19 +268,19 @@
     def own_sends(whole):
         mine = big(y, x) if whole else small(y, x)
         if whole:
-            return [copy(mine, mine, S_Y + k, device(x, h, (y + k) % NY, l, c)) for k in NEAR]
-        return [copy(mine, mine, S_BX + k, device((x + k) % NX, h, y, l, c)) for k in (1, 3, 2)]
+            return [copy(mine, mine, S_Y + k, device(x, h, ys_at[k], l, c)) for k in NEAR]
+        return [copy(mine, mine, S_BX + k, device(xs_at[k], h, y, l, c)) for k in (1, 3, 2)]
 
     def cross_sends(whole):
         mine = big(y, x) if whole else small(y, x)
         sends = []
         for k in (0, *NEAR) if whole else (0, 1, 3, 2):
             for m in range(2):
-                ll = (3 - m) * (1 - l // 3) + m * (l // 3)
+                ll = cross_l[m]
                 if whole:
-                    to, slot = device(x, 1 - h, (y + k) % NY, ll, c), S_Y + k
+                    to, slot = device(x, hs_at[1], ys_at[k], ll, c), S_Y + k
                 else:
-                    to, slot = device((x + k) % NX, 1 - h, y, ll, c), S_BX + k
+                    to, slot = device(xs_at[k], hs_at[1], y, ll, c), S_BX + k
                 sends.append(
                     pltpu.make_async_remote_copy(
                         src_ref=mine, dst_ref=mine, send_sem=ssem.at[S_C + 2 * k + m], recv_sem=rsem.at[slot],
@@ -268,23 +290,23 @@
         return sends
 
     def x_sends(k):
-        ref = big((y - k + NY) % NY, x)
-        return [copy(ref, ref, S_X + 3 * k + dx - 1, device((x + dx) % NX, h, y, l, c)) for dx in (2, 1, 3)]
+        ref = big(ys_at[-k % NY], x)
+        return [copy(ref, ref, S_X + 3 * k + dx - 1, device(xs_at[dx], h, y, l, c)) for dx in (2, 1, 3)]
 
     def forward(k, whole):
         if k or not whole:
-            arrived(big((y - k + NY) % NY, x), S_Y + k)
+            arrived(big(ys_at[-k % NY], x), S_Y + k)
         for each in x_sends(k):
             each.start()
 
     def small_sends():
         ref = w.at[y, :, 0:2]
-        return [copy(ref, ref, S_BY + k, device(x, h, (y + k) % NY, l, c)) for k in (4, 3, 5, 2, 6, 1, 7)]
+        return [copy(ref, ref, S_BY + k, device(x, h, ys_at[k], l, c)) for k in (4, 3, 5, 2, 6, 1, 7)]
 
     def forward_small(whole):
         for k in range(NX):
             if k or whole:
-                arrived(small(y, (x - k + NX) % NX), S_BX + k)
+                arrived(small(y, xs_at[-k % NX]), S_BX + k)
         for each in small_sends():
             each.start()
 
@@ -306,7 +328,7 @@
     kg1 = []
     for k in range(1, 8):
         dx, dh = k // 2, k % 2
-        each = copy(kg_own, kg_xh.at[k], S_KG1 + k, device((x + dx) % NX, (h + dh) % NH, y, l, c))
+        each = copy(kg_own, kg_xh.at[k], S_KG1 + k, device(xs_at[dx], hs_at[dh], y, l, c))
         each.start()
         kg1.append(each)
 
@@ -340,8 +362,6 @@
         for k in (2, 6) if whole else (1, 7):
             forward(k, whole)
         forward_small(whole)
-        for k in (3, 5) if whole else (2, 6):
-            forward(k, whole)
 
     both(third_leg)
 
@@ -354,18 +374,18 @@
     kg2 = []
     for k in range(1, NY):
         mine = kg_all.at[y]
-        each = copy(mine, mine, S_KG2 + k, device(x, h, (y + k) % NY, l, c))
+        each = copy(mine, mine, S_KG2 + k, device(x, h, ys_at[k], l, c))
         each.start()
         kg2.append(each)
 
     def fourth_leg(whole):
-        for k in (4,) if whole else (3, 5, 4):
+        for k in (3, 5, 4) if whole else (2, 6, 3, 5, 4):
             forward(k, whole)
 
     both(fourth_leg)
 
     for k in range(1, NY):
-        arrived(kg_all.at[(y - k + NY) % NY], S_KG2 + k)
+        arrived(kg_all.at[ys_at[-k % NY]], S_KG2 + k)
     rows64 = lax.broadcasted_iota(jnp.int32, (64, 256), 0)
     chan = lax.broadcasted_iota(jnp.int32, (64, 256), 1)
     owner = (chan // 4) == ((rows64 % 8) * 8 + rows64 // 8)
@@ -413,11 +433,12 @@
         rstd[at, :] = jnp.broadcast_to(inv, (64, 128))
         normed = hat * krows[9:10, :]
         norm_own[at, :] = normed
+        copy(norm_own.at[at], norm_sib.at[at], S_NORM + r, sibling).start()
         return carry
 
     lax.fori_loop(0, 4, conv_rows, 0)
-    norm_copy = copy(norm_own, norm_sib, S_NORM, sibling)
-    norm_copy.start()
+    parts = [pl.ds(64 * r, 64) for r in range(4)]
+    norm_copies = [copy(norm_own.at[at], norm_sib.at[at], S_NORM + r, sibling) for r, at in enumerate(parts)]
 
     def prepare_tokens(m, source):
         def halves(r, carry):
@@ -436,10 +457,10 @@
     prepare_tokens(0, norm_own)
 
     for k in NEAR:
-        arrived(w.at[(y - k + NY) % NY, :, 0:2], S_BY + k)
+        arrived(w.at[ys_at[-k % NY], :, 0:2], S_BY + k)
     for k in (0, *NEAR):
         for dx in (1, 3, 2):
-            arrived(big((y - k + NY) % NY, (x - dx + NX) % NX), S_X + 3 * k + dx - 1)
+            arrived(big(ys_at[-k % NY], xs_at[-dx % NX]), S_X + 3 * k + dx - 1)
 
     lows = lax.broadcasted_iota(jnp.int32, (4, 8, 128), 1) < 4
 
@@ -477,48 +498,54 @@
         return carry
 
     lax.fori_loop(0, 4, prepare_cot, 0)
-    arrived(norm_sib, S_NORM)
-    prepare_tokens(1, norm_sib)
-
-    def first_products(e, carry):
+    def first_products(e, m):
         downs = (d_hi[e], d_lo[e])
-        ups = (u_hi[e], u_lo[e])
-        total = jnp.zeros((256, 256), F32)
-        for m in range(2):
-            grads = (g_hi[m], g_lo[m])
-            pre = dot3((n_hi[m], n_lo[m]), ups, NN)
-            back = dot3(grads, downs, NT)
-            square = pre * pre
-            t = jnp.tanh(ROOT * (pre + 0.044715 * (square * pre)))
-            half = 0.5 * (1.0 + t)
-            hidden = pre * half
-            slope = half + 0.5 * pre * (1.0 - t * t) * (ROOT * (1.0 + 3 * 0.044715 * square))
-            high, low = split(back * slope)
-            p_hi[m, e] = high
-            p_lo[m, e] = low
-            high, low = split(hidden)
-            h_hi[m, e] = high
-            h_lo[m, e] = low
-            total = total + dot3(split(jnp.transpose(hidden)), grads, NN)
+        grads = (g_hi[m], g_lo[m])
+        pre = dot3((n_hi[m], n_lo[m]), (u_hi[e], u_lo[e]), NN)
+        back = dot3(grads, downs, NT)
+        square = pre * pre
+        t = jnp.tanh(ROOT * (pre + 0.044715 * (square * pre)))
+        half = 0.5 * (1.0 + t)
+        hidden = pre * half
+        slope = half + 0.5 * pre * (1.0 - t * t) * (ROOT * (1.0 + 3 * 0.044715 * square))
+        high, low = split(back * slope)
+        p_hi[m, e] = high
+        p_lo[m, e] = low
+        high, low = split(hidden)
+        h_hi[m, e] = high
+        h_lo[m, e] = low
+        value = dot3(split(jnp.transpose(hidden)), grads, NN)
+        dgrad[...] = value if m == 0 else dgrad[...] + value
+
+    def x_reduce(first, count, into, base):
+        return [
+            copy(
+                g.at[pl.ds(4 * yh, 4), xs_at[dx], pl.ds(first, count)], into.at[dx - 1, pl.ds(4 * yh, 4)],
+                base + 3 * yh + dx - 1, device(xs_at[dx], h, y, l, c),
+            )
+            for yh in range(2)
+            for dx in (2, 1, 3)
+        ]
+
+    reduces = x_reduce(4, 4, x_recv, R_X)
+    for e in range(2):
+        first_products(e, 0)
+        if e == 0:
+            for r, at in enumerate(parts):
+                arrived(norm_sib.at[at], S_NORM + r)
+            prepare_tokens(1, norm_sib)
+        first_products(e, 1)
         for bb in range(2):
             for q in range(2):
-                v = total[128 * bb : 128 * bb + 128, 128 * q : 128 * q + 128].reshape(8, 2, 8, 128)
+                v = dgrad[128 * bb : 128 * bb + 128, 128 * q : 128 * q + 128].reshape(8, 2, 8, 128)
                 for rh in range(2):
                     g[:, 2 * e + bb, 4 + 2 * rh + q] = v[:, rh]
-        return carry
-
-    lax.fori_loop(0, 2, first_products, 0)
-
-    reduces = []
-    for k, offset in enumerate(FAR):
-        yy = (y + offset) % NY
-        for dx in (2, 1, 3):
-            to = (x + dx) % NX
-            each = copy(
-                g.at[yy, to, 4:8], x_recv.at[k, dx - 1], R_X + 3 * k + dx - 1, device(to, h, y, l, c)
-            )
-            each.start()
-            reduces.append(each)
+        for k, dx in enumerate((2, 1, 3)):
+
+            @pl.when(xs_at[dx] // 2 == e)
+            def _(k=k):
+                reduces[k].start()
+                reduces[3 + k].start()
 
     def second_products(e, carry):
         ugrad[e] = sum(
@@ -544,19 +571,13 @@
 
     lax.fori_loop(0, NX, pack, 0)
     for k in (4, 3, 5, 2, 6, 1, 7):
-        yy = (y + k) % NY
+        yy = ys_at[k]
         each = copy(g.at[yy, :, 0:2], by_recv.at[k], R_BY + k, device(x, h, yy, l, c))
         each.start()
         reduces.append(each)
-    for k, offset in enumerate(FAR):
-        yy = (y + offset) % NY
-        for dx in (2, 1, 3):
-            to = (x + dx) % NX
-            each = copy(
-                g.at[yy, to, 2:4], xu_recv.at[k, dx - 1], R_XU + 3 * k + dx - 1, device(to, h, y, l, c)
-            )
-            each.start()
-            reduces.append(each)
+    for each in x_reduce(2, 2, xu_recv, R_XU):
+        each.start()
+        reduces.append(each)
 
     swaps = [copy(dnorm.at[1], dn_recv, R_BR, sibling), copy(branch.at[1], br_recv, R_BR + 1, sibling)]
     for m in (1, 0):
@@ -635,7 +656,7 @@
     kgr_own[...] = folded.reshape(8, 8, 128)
     kgs = []
     for k in range(1, NY):
-        yy = (y + k) % NY
+        yy = ys_at[k]
         each = copy(kgr_own.at[yy], kgr_y.at[k], R_KY + k, device(x, h, yy, l, c))
         each.start()
         kgs.append(each)
@@ -647,22 +668,27 @@
         total = total + by_recv[k]
     g[y, :, 0:2] = total
     for dx in (2, 1, 3):
-        to = (x + dx) % NX
+        to = xs_at[dx]
         each = copy(g.at[y, to, 0:2], bx_recv.at[dx], R_BX + dx, device(to, h, y, l, c))
         each.start()
         reduces.append(each)
 
-    for k, offset in enumerate(FAR):
-        yy = (y + offset) % NY
+    for yh in range(2):
+        half = pl.ds(4 * yh, 4)
         for dx in (1, 3, 2):
-            arrived(x_recv.at[k, dx - 1], R_X + 3 * k + dx - 1)
-            arrived(xu_recv.at[k, dx - 1], R_XU + 3 * k + dx - 1)
-        g[yy, x, 4:8] = (g[yy, x, 4:8] + x_recv[k, 0]) + (x_recv[k, 1] + x_recv[k, 2])
-        g[yy, x, 2:4] = (g[yy, x, 2:4] + xu_recv[k, 0]) + (xu_recv[k, 1] + xu_recv[k, 2])
-        if offset:
-            each = copy(g.at[yy, x, 2:8], y_recv.at[offset], R_Y + offset, device(x, h, yy, l, c))
-            each.start()
-            reduces.append(each)
+            arrived(x_recv.at[dx - 1, half], R_X + 3 * yh + dx - 1)
+            arrived(xu_recv.at[dx - 1, half], R_XU + 3 * yh + dx - 1)
+        g[half, x, 4:8] = (g[half, x, 4:8] + x_recv[0, half]) + (x_recv[1, half] + x_recv[2, half])
+        g[half, x, 2:4] = (g[half, x, 2:4] + xu_recv[0, half]) + (xu_recv[1, half] + xu_recv[2, half])
+        for k in range(1, NY):
+            yy = ys_at[k]
+
+            @pl.when(yy // 4 == yh)
+            def _(k=k, yy=yy):
+                copy(g.at[yy, x, 2:8], y_recv.at[k], R_Y + k, device(x, h, yy, l, c)).start()
+
+    for k in range(1, NY):
+        reduces.append(copy(g.at[ys_at[k], x, 2:8], y_recv.at[k], R_Y + k, device(x, h, ys_at[k], l, c)))
 
     arrived(br_recv, R_BR + 1)
 
@@ -696,7 +722,7 @@
         total = total + kgr_y[k]
     kgr_x[x] = total
     for k in range(1, NX):
-        each = copy(kgr_x.at[x], kgr_x.at[x], R_KX + k, device((x + k) % NX, h, y, l, c))
+        each = copy(kgr_x.at[x], kgr_x.at[x], R_KX + k, device(xs_at[k], h, y, l, c))
         each.start()
         kgs.append(each)
 
@@ -716,7 +742,7 @@
             dh, dl = k // 4, k % 4
             full = whole if dh == 0 else not whole
             ref = z_recv.at[z, 2:8] if full else z_recv.at[z, 0:2]
-            sends.append(copy(ref, ref, R_Z + k, device(x, (h + dh) % NH, y, (l + dl) % NL, c)))
+            sends.append(copy(ref, ref, R_Z + k, device(x, hs_at[dh], y, ls_at[dl], c)))
         return sends
 
     def z_start(whole):
@@ -726,14 +752,14 @@
     both(z_start)
 
     for k in range(1, NX):
-        arrived(kgr_x.at[(x - k + NX) % NX], R_KX + k)
+        arrived(kgr_x.at[xs_at[-k % NX]], R_KX + k)
     total = kgr_x[0]
     for k in range(1, NX):
         total = total + kgr_x[k]
     zc = z * 2 + c
     kgr_z[zc] = total
     for k in range(1, 16):
-        to = device(x, (h + k // 8) % 2, y, (l + (k // 2) % 4) % 4, (c + k % 2) % 2)
+        to = device(x, hs_at[k // 8], y, ls_at[(k // 2) % 4], cs_at[k % 2])
         each = copy(kgr_z.at[zc], kgr_z.at[zc], R_KZ + k, to)
         each.start()
         kgs.append(each)
@@ -747,6 +773,22 @@
     stores.append(pltpu.make_async_copy(out_field, field_out, rsem.at[S_OUT + 1]))
     stores[1].start()
 
+    def early_sent(whole):
+        for each in own_sends(whole):
+            each.wait_send()
+
+        @pl.when(ends == 0)
+        def _():
+            for each in cross_sends(whole):
+                each.wait_send()
+
+    both(early_sent)
+    for k in range(NY):
+        for each in x_sends(k):
+            each.wait_send()
+    for each in [*small_sends(), *we, *kg1, *ns, *kg2, cot_copy, *norm_copies, *swaps, *reduces, *bns]:
+        each.wait_send()
+
     def fin_sends(whole):
         sends = [copy(fin_up.at[c], fin_up.at[c], R_F, sibling)]
         if whole:
@@ -755,7 +797,7 @@
 
     def z_end(whole):
         for k in range(1, 8):
-            zz = ((h + k // 4) % NH) * 4 + (l - k % 4 + NL) % NL
+            zz = (hs_at[k // 4]) * 4 + ls_at[-(k % 4) % NL]
             arrived(z_recv.at[zz, 2:8] if whole else z_recv.at[zz, 0:2], R_Z + k)
         span = slice(2, 8) if whole else slice(0, 2)
         total = z_recv[0, span]
@@ -786,7 +828,7 @@
     stores[3].start()
 
     for k in range(1, 16):
-        hh, ll, cc = (h + k // 8) % 2, (l - (k // 2) % 4 + 4) % 4, (c + k % 2) % 2
+        hh, ll, cc = hs_at[k // 8], ls_at[-(k // 2) % 4], cs_at[k % 2]
         arrived(kgr_z.at[(hh * 4 + ll) * 2 + cc], R_KZ + k)
     total = kgr_z[0]
     for k in range(1, 16):
@@ -795,22 +837,12 @@
     stores.append(pltpu.make_async_copy(out_kg, kg_out, rsem.at[S_OUT + 4]))
     stores[4].start()
 
-    def all_sent(whole):
-        for each in own_sends(whole) + z_sends(whole) + fin_sends(whole):
+    def last_sent(whole):
+        for each in z_sends(whole) + fin_sends(whole):
             each.wait_send()
 
-        @pl.when(ends == 0)
-        def _():
-            for each in cross_sends(whole):
-                each.wait_send()
-
-    both(all_sent)
-    for k in range(NY):
-        for each in x_sends(k):
-            each.wait_send()
-    for each in [
-        *small_sends(), *we, *kg1, *ns, *kg2, cot_copy, norm_copy, *swaps, *reduces, *bns, *kgs, *bwe
-    ]:
+    both(last_sent)
+    for each in [*kgs, *bwe]:
         each.wait_send()
     for each in stores:
         each.wait()
@@ -880,8 +912,8 @@
             half(2, 256, 256), half(2, 256, 256),
             half(2, 2, 256, 256), half(2, 2, 256, 256), half(2, 2, 256, 256), half(2, 2, 256, 256),
             buf(2, 256, 256), buf(2, 256, 256), buf(256, 256), buf(256, 256),
-            buf(2, 256, 256), buf(2, 256, 256), buf(16, 256),
-            buf(8, 3, 4, 8, 128), buf(8, 3, 2, 8, 128), buf(8, 6, 8, 128),
+            buf(2, 256, 256), buf(256, 256), buf(16, 256),
+            buf(3, 8, 4, 8, 128), buf(3, 8, 2, 8, 128), buf(8, 6, 8, 128),
             buf(8, 4, 2, 8, 128), buf(4, 2, 8, 128), buf(8, 8, 8, 128),
             buf(2, 2, 8, 128), buf(4, 8, 128),
             pltpu.SemaphoreType.DMA((N_SLOTS,)),

time: 69.9 us -> 66.7 us (0.954)
  Pallas kernels: 69.1 us -> 65.9 us
    pallas_call x1, Pallas kernels: 67.2 us -> 64.1 us  [shards(): pl.pallas_call(kernel, out_shape=(jax.ShapeDtypeStruct((16, 16, 256), F32...]
where the time goes in v4:
time: 66.7 us; the launch traced here: 66.6 us
  Pallas kernels  65.9 us (99%)
    pallas_call x1, Pallas kernels, shards(): pl.pallas_call(kernel, out_shape=(jax.ShapeDtypeStruct((16, 16, 256), F32...  64.1 us
    pallas_call x1, Pallas kernels, shards(): pl.pallas_call(results, out_shape=(jax.ShapeDtypeStruct((16, 16, 256), F3...  1.85 us

profile of v4, /device:TPU:1, one launch (start us, length us, event | category | flops | bytes accessed | tf_op | source)
XLA Modules:
  0.0 66.6 jit_solution(6924036936551974533)
XLA Ops:
  0.6 64.1 %block.1 = (f32[16,16,256]{2,1,0:T(8,128)}, f32[16,16,256]{2,1,0:T(8,128)}, f32[4,1024]{1,0:T(4,128)}, f32[16,256]{1,0:T(8,128)}, f32[1,128]{1,0:T(1,128)}) custom-call(f32[16,16,256]{2,1,0:T(8,128)} %bitcast.9, f32[16,16,256]{2,1,0:T(8,128)} %bitcast.10, f32[4,1024]{1,0:T(4,128)} %up_in.1, f32[16,256]{1,0:T(8,128)} %down_in.1, f32[4,9]{1,0:T(4,128)} %bitcast.11, ...), custom_call_target="tpu_custom_call" | custom-call | tf_op jit(solution)/shard_map/block/pallas_call | solution.py:888
  64.7 1.8 %results.1 = (f32[16,16,256]{2,1,0:T(8,128)}, f32[16,16,256]{2,1,0:T(8,128)}, f32[4,1024]{1,0:T(4,128)}, f32[16,256]{1,0:T(8,128)}, f32[4,9]{1,0:T(4,128)}, /*index=5*/f32[1,4]{1,0:T(1,128)}) custom-call(f32[16,16,256]{2,1,0:T(8,128)} %get-tuple-element.17.new, f32[16,16,256]{2,1,0:T(8,128)} %get-tuple-element.18.field, f32[4,1024]{1,0:T(4,128)} %get-tuple-element.19.up, ...), custom_call_target="tpu_custom_call" | custom-call | tf_op jit(solution)/shard_map/results/pallas_call | solution.py:930

commit v5 on v4

--- a/solution.py
+++ b/solution.py
@@ -29,7 +29,8 @@
 
 SLOTS = Slots()
 S_Y = SLOTS.take(8)
-S_C = SLOTS.take(16)
+S_C = SLOTS.take(8)
+S_CK = SLOTS.take(8)
 S_X = SLOTS.take(24)
 S_BX = SLOTS.take(8)
 S_BY = SLOTS.take(8)
@@ -141,8 +142,8 @@
     for k in range(1, NY):
         peers.append(device(x, h, ys_at[k], l, c))
     for dx in range(1, NX):
-        for dh in range(NH):
-            peers.append(device(xs_at[dx], hs_at[dh], y, l, c))
+        peers.append(device(xs_at[dx], h, y, l, c))
+    peers.append(device((x + 2 * h + 3) % NX, hs_at[1], y, l, c))
     loads = [
         pltpu.make_async_copy(src, dst, ssem.at[S_IN + k])
         for k, (src, dst) in enumerate(
@@ -157,15 +158,8 @@
 
     for peer in peers:
         greet(peer)
-    def greet_sources(whole):
-        if whole:
-            for k in range(NX):
-                greet(device(xs_at[k], hs_at[1], y, source, c))
-        else:
-            for k in range(NY):
-                greet(device(x, hs_at[1], ys_at[k], source, c))
-
-    both(greet_sources)
+    for k in range(NX):
+        greet(device(xs_at[k], hs_at[1], y, source, c))
     for each in loads:
         each.wait()
 
@@ -253,7 +247,7 @@
 
     lax.fori_loop(0, 4, prepare, 0)
 
-    pl.semaphore_wait(barrier, len(peers) + (1 - ends) * (16 - 8 * same))
+    pl.semaphore_wait(barrier, len(peers) + (1 - ends) * 8)
 
     we = rim_copies(we_send, we_recv, S_HALO, 1, 2, 3, inner_w, inner_e)
     for each in we:
@@ -268,33 +262,39 @@
     def own_sends(whole):
         mine = big(y, x) if whole else small(y, x)
         if whole:
-            return [copy(mine, mine, S_Y + k, device(x, h, ys_at[k], l, c)) for k in NEAR]
+            return y_sends()
         return [copy(mine, mine, S_BX + k, device(xs_at[k], h, y, l, c)) for k in (1, 3, 2)]
 
     def cross_sends(whole):
         mine = big(y, x) if whole else small(y, x)
         sends = []
-        for k in (0, *NEAR) if whole else (0, 1, 3, 2):
+        for k in (0,) if whole else (0, 1, 3, 2):
             for m in range(2):
-                ll = cross_l[m]
-                if whole:
-                    to, slot = device(x, hs_at[1], ys_at[k], ll, c), S_Y + k
-                else:
-                    to, slot = device(xs_at[k], hs_at[1], y, ll, c), S_BX + k
                 sends.append(
-                    pltpu.make_async_remote_copy(
-                        src_ref=mine, dst_ref=mine, send_sem=ssem.at[S_C + 2 * k + m], recv_sem=rsem.at[slot],
-                        device_id=to, device_id_type=MESH,
+                    copy(
+                        mine, mine, S_Y if whole else S_BX + k, device(xs_at[k], hs_at[1], y, cross_l[m], c),
+                        S_C + 2 * k + m,
                     )
                 )
         return sends
 
+    def y_sends():
+        ref = big(y, x)
+        return [copy(ref, ref, S_Y + k, device(x, h, ys_at[k], l, c)) for k in NEAR]
+
+    def kg_cross():
+        return [
+            copy(kg_own, kg_xh.at[4 + k], S_KG1 + 4 + k, device(xs_at[k], hs_at[1], y, cross_l[m], c), S_CK + 2 * k + m)
+            for k in (0, 1, 3, 2)
+            for m in range(2)
+        ]
+
     def x_sends(k):
         ref = big(ys_at[-k % NY], x)
         return [copy(ref, ref, S_X + 3 * k + dx - 1, device(xs_at[dx], h, y, l, c)) for dx in (2, 1, 3)]
 
     def forward(k, whole):
-        if k or not whole:
+        if k:
             arrived(big(ys_at[-k % NY], x), S_Y + k)
         for each in x_sends(k):
             each.start()
@@ -325,19 +325,23 @@
     both(first_leg)
     cot_copy = copy(cot, cot_sib, S_COT, sibling)
     cot_copy.start()
-    kg1 = []
-    for k in range(1, 8):
-        dx, dh = k // 2, k % 2
-        each = copy(kg_own, kg_xh.at[k], S_KG1 + k, device(xs_at[dx], hs_at[dh], y, l, c))
-        each.start()
-        kg1.append(each)
+    kg1 = [copy(kg_own, kg_xh.at[k], S_KG1 + k, device(xs_at[k], h, y, l, c)) for k in range(1, NX)]
+    for each in kg1:
+        each.start()
+
+    @pl.when(ends == 0)
+    def _():
+        for each in kg_cross():
+            each.start()
 
     def second_leg(whole):
         if whole:
             forward(1, whole)
             forward(7, whole)
         else:
-            forward(0, whole)
+            arrived(big(y, x), S_Y)
+            for each in y_sends() + x_sends(0):
+                each.start()
 
     both(second_leg)
 
@@ -358,13 +362,6 @@
     for each in ns:
         each.start()
 
-    def third_leg(whole):
-        for k in (2, 6) if whole else (1, 7):
-            forward(k, whole)
-        forward_small(whole)
-
-    both(third_leg)
-
     for k in range(1, 8):
         arrived(kg_xh.at[k], S_KG1 + k)
     total = kg_xh[0]
@@ -378,8 +375,15 @@
         each.start()
         kg2.append(each)
 
+    def third_leg(whole):
+        for k in (2, 6) if whole else ():
+            forward(k, whole)
+        forward_small(whole)
+
+    both(third_leg)
+
     def fourth_leg(whole):
-        for k in (3, 5, 4) if whole else (2, 6, 3, 5, 4):
+        for k in (3, 5, 4) if whole else NEAR:
             forward(k, whole)
 
     both(fourth_leg)
@@ -774,12 +778,12 @@
     stores[1].start()
 
     def early_sent(whole):
-        for each in own_sends(whole):
+        for each in own_sends(whole) + ([] if whole else y_sends()):
             each.wait_send()
 
         @pl.when(ends == 0)
         def _():
-            for each in cross_sends(whole):
+            for each in cross_sends(whole) + kg_cross():
                 each.wait_send()
 
     both(early_sent)

time: 66.7 us -> 65 us (0.975)
  Pallas kernels: 65.9 us -> 63.9 us
    pallas_call x1, Pallas kernels: 64.1 us -> 62 us  [shards(): pl.pallas_call(kernel, out_shape=(jax.ShapeDtypeStruct((16, 16, 256), F32...]
where the time goes in v5:
time: 65 us; the launch traced here: 64.5 us
  Pallas kernels  63.9 us (98%)
    pallas_call x1, Pallas kernels, shards(): pl.pallas_call(kernel, out_shape=(jax.ShapeDtypeStruct((16, 16, 256), F32...  62 us
    pallas_call x1, Pallas kernels, shards(): pl.pallas_call(results, out_shape=(jax.ShapeDtypeStruct((16, 16, 256), F3...  1.85 us

profile of v5, /device:TPU:1, one launch (start us, length us, event | category | flops | bytes accessed | tf_op | source)
XLA Modules:
  0.0 64.5 jit_solution(8290146799446878986)
XLA Ops:
  0.6 62.0 %block.1 = (f32[16,16,256]{2,1,0:T(8,128)}, f32[16,16,256]{2,1,0:T(8,128)}, f32[4,1024]{1,0:T(4,128)}, f32[16,256]{1,0:T(8,128)}, f32[1,128]{1,0:T(1,128)}) custom-call(f32[16,16,256]{2,1,0:T(8,128)} %bitcast.9, f32[16,16,256]{2,1,0:T(8,128)} %bitcast.10, f32[4,1024]{1,0:T(4,128)} %up_in.1, f32[16,256]{1,0:T(8,128)} %down_in.1, f32[4,9]{1,0:T(4,128)} %bitcast.11, ...), custom_call_target="tpu_custom_call" | custom-call | tf_op jit(solution)/shard_map/block/pallas_call | solution.py:892
  62.7 1.8 %results.1 = (f32[16,16,256]{2,1,0:T(8,128)}, f32[16,16,256]{2,1,0:T(8,128)}, f32[4,1024]{1,0:T(4,128)}, f32[16,256]{1,0:T(8,128)}, f32[4,9]{1,0:T(4,128)}, /*index=5*/f32[1,4]{1,0:T(1,128)}) custom-call(f32[16,16,256]{2,1,0:T(8,128)} %get-tuple-element.17.new, f32[16,16,256]{2,1,0:T(8,128)} %get-tuple-element.18.field, f32[4,1024]{1,0:T(4,128)} %get-tuple-element.19.up, ...), custom_call_target="tpu_custom_call" | custom-call | tf_op jit(solution)/shard_map/results/pallas_call | solution.py:934

commit v6 on v5

--- a/solution.py
+++ b/solution.py
@@ -147,7 +147,7 @@
     loads = [
         pltpu.make_async_copy(src, dst, ssem.at[S_IN + k])
         for k, (src, dst) in enumerate(
-            ((state_in, state), (kt_in, kt), (gn_in, gn), (up_in, up), (down_in, down), (cot_in, cot))
+            ((up_in, up), (down_in, down), (kt_in, kt), (gn_in, gn), (state_in, state), (cot_in, cot))
         )
     ]
     for each in loads:
@@ -160,7 +160,7 @@
         greet(peer)
     for k in range(NX):
         greet(device(xs_at[k], hs_at[1], y, source, c))
-    for each in loads:
+    for each in loads[:2]:
         each.wait()
 
     def own_up(core, first):
@@ -183,6 +183,8 @@
 
             pl.when((c * 2 + same) == (core * 2 + kind))(own)
 
+    for each in loads[2:4]:
+        each.wait()
     sub8 = lax.broadcasted_iota(jnp.int32, (8, 128), 0)
     kg_row[...] = jnp.zeros_like(kg_row)
     for i in range(4):
@@ -200,6 +202,7 @@
     def mixed(flip, a, b):
         return a * (1.0 - flip) + b * flip
 
+    loads[4].wait()
     for i in range(16):
         we_send[0, i : i + 1, :] = mixed(flips[2], state[i, 0:1, :], state[15 - i, 0:1, :])
         we_send[1, i : i + 1, :] = mixed(flips[3], state[i, 15:16, :], state[15 - i, 15:16, :])
@@ -233,20 +236,6 @@
         )
         return low, high
 
-    def prepare(r, carry):
-        rows = state[pl.ds(r * 4, 4)]
-        at = pl.ds(1 + r * 4, 4)
-        middle[at] = rows
-        west[at] = pltpu.roll(rows, 1, 1)
-        east[at] = pltpu.roll(rows, 15, 1)
-        high, low = split(cot[pl.ds(r * 4, 4)].reshape(64, 256))
-        to = pl.ds(pl.multiple_of(r * 64, 64), 64)
-        g_hi[0, to, :] = high
-        g_lo[0, to, :] = low
-        return carry
-
-    lax.fori_loop(0, 4, prepare, 0)
-
     pl.semaphore_wait(barrier, len(peers) + (1 - ends) * 8)
 
     we = rim_copies(we_send, we_recv, S_HALO, 1, 2, 3, inner_w, inner_e)
@@ -323,8 +312,6 @@
             forward(0, whole)
 
     both(first_leg)
-    cot_copy = copy(cot, cot_sib, S_COT, sibling)
-    cot_copy.start()
     kg1 = [copy(kg_own, kg_xh.at[k], S_KG1 + k, device(xs_at[k], h, y, l, c)) for k in range(1, NX)]
     for each in kg1:
         each.start()
@@ -333,6 +320,24 @@
     def _():
         for each in kg_cross():
             each.start()
+
+    loads[5].wait()
+    cot_copy = copy(cot, cot_sib, S_COT, sibling)
+    cot_copy.start()
+
+    def prepare(r, carry):
+        rows = state[pl.ds(r * 4, 4)]
+        at = pl.ds(1 + r * 4, 4)
+        middle[at] = rows
+        west[at] = pltpu.roll(rows, 1, 1)
+        east[at] = pltpu.roll(rows, 15, 1)
+        high, low = split(cot[pl.ds(r * 4, 4)].reshape(64, 256))
+        to = pl.ds(pl.multiple_of(r * 64, 64), 64)
+        g_hi[0, to, :] = high
+        g_lo[0, to, :] = low
+        return carry
+
+    lax.fori_loop(0, 4, prepare, 0)
 
     def second_leg(whole):
         if whole:
@@ -437,28 +442,15 @@
         rstd[at, :] = jnp.broadcast_to(inv, (64, 128))
         normed = hat * krows[9:10, :]
         norm_own[at, :] = normed
+        high, low = split(normed)
+        n_hi[0, at, :] = high
+        n_lo[0, at, :] = low
         copy(norm_own.at[at], norm_sib.at[at], S_NORM + r, sibling).start()
         return carry
 
     lax.fori_loop(0, 4, conv_rows, 0)
     parts = [pl.ds(64 * r, 64) for r in range(4)]
     norm_copies = [copy(norm_own.at[at], norm_sib.at[at], S_NORM + r, sibling) for r, at in enumerate(parts)]
-
-    def prepare_tokens(m, source):
-        def halves(r, carry):
-            at = pl.ds(pl.multiple_of(r * 128, 128), 128)
-            value = source[at, :]
-            high, low = split(value)
-            n_hi[m, at, :] = high
-            n_lo[m, at, :] = low
-            high, low = split(jnp.transpose(value))
-            nt_hi[m, r] = high
-            nt_lo[m, r] = low
-            return carry
-
-        lax.fori_loop(0, 2, halves, 0)
-
-    prepare_tokens(0, norm_own)
 
     for k in NEAR:
         arrived(w.at[ys_at[-k % NY], :, 0:2], S_BY + k)
@@ -537,7 +529,10 @@
         if e == 0:
             for r, at in enumerate(parts):
                 arrived(norm_sib.at[at], S_NORM + r)
-            prepare_tokens(1, norm_sib)
+            for r in range(4):
+                high, low = split(norm_sib[64 * r : 64 * r + 64, :])
+                n_hi[1, 64 * r : 64 * r + 64, :] = high
+                n_lo[1, 64 * r : 64 * r + 64, :] = low
         first_products(e, 1)
         for bb in range(2):
             for q in range(2):
@@ -550,6 +545,12 @@
             def _(k=k):
                 reduces[k].start()
                 reduces[3 + k].start()
+
+    for m, source_ref in enumerate((norm_own, norm_sib)):
+        for r in range(2):
+            high, low = split(jnp.transpose(source_ref[128 * r : 128 * r + 128, :]))
+            nt_hi[m, r] = high
+            nt_lo[m, r] = low
 
     def second_products(e, carry):
         ugrad[e] = sum(
@@ -574,12 +575,12 @@
         return carry
 
     lax.fori_loop(0, NX, pack, 0)
+    for each in x_reduce(2, 2, xu_recv, R_XU):
+        each.start()
+        reduces.append(each)
     for k in (4, 3, 5, 2, 6, 1, 7):
         yy = ys_at[k]
         each = copy(g.at[yy, :, 0:2], by_recv.at[k], R_BY + k, device(x, h, yy, l, c))
-        each.start()
-        reduces.append(each)
-    for each in x_reduce(2, 2, xu_recv, R_XU):
         each.start()
         reduces.append(each)
 
@@ -665,17 +666,21 @@
         each.start()
         kgs.append(each)
 
-    for k in range(1, NY):
-        arrived(by_recv.at[k], R_BY + k)
-    total = g[y, :, 0:2]
-    for k in range(1, NY):
-        total = total + by_recv[k]
-    g[y, :, 0:2] = total
-    for dx in (2, 1, 3):
-        to = xs_at[dx]
-        each = copy(g.at[y, to, 0:2], bx_recv.at[dx], R_BX + dx, device(to, h, y, l, c))
-        each.start()
-        reduces.append(each)
+    def early_sent(whole):
+        for each in own_sends(whole) + ([] if whole else y_sends()):
+            each.wait_send()
+
+        @pl.when(ends == 0)
+        def _():
+            for each in cross_sends(whole) + kg_cross():
+                each.wait_send()
+
+    both(early_sent)
+    for k in range(NY):
+        for each in x_sends(k):
+            each.wait_send()
+    for each in [*small_sends(), *we, *kg1, *ns, *kg2, cot_copy, *norm_copies]:
+        each.wait_send()
 
     for yh in range(2):
         half = pl.ds(4 * yh, 4)
@@ -693,6 +698,18 @@
 
     for k in range(1, NY):
         reduces.append(copy(g.at[ys_at[k], x, 2:8], y_recv.at[k], R_Y + k, device(x, h, ys_at[k], l, c)))
+
+    for k in range(1, NY):
+        arrived(by_recv.at[k], R_BY + k)
+    total = g[y, :, 0:2]
+    for k in range(1, NY):
+        total = total + by_recv[k]
+    g[y, :, 0:2] = total
+    for dx in (2, 1, 3):
+        to = xs_at[dx]
+        each = copy(g.at[y, to, 0:2], bx_recv.at[dx], R_BX + dx, device(to, h, y, l, c))
+        each.start()
+        reduces.append(each)
 
     arrived(br_recv, R_BR + 1)
 
@@ -777,20 +794,7 @@
     stores.append(pltpu.make_async_copy(out_field, field_out, rsem.at[S_OUT + 1]))
     stores[1].start()
 
-    def early_sent(whole):
-        for each in own_sends(whole) + ([] if whole else y_sends()):
-            each.wait_send()
-
-        @pl.when(ends == 0)
-        def _():
-            for each in cross_sends(whole) + kg_cross():
-                each.wait_send()
-
-    both(early_sent)
-    for k in range(NY):
-        for each in x_sends(k):
-            each.wait_send()
-    for each in [*small_sends(), *we, *kg1, *ns, *kg2, cot_copy, *norm_copies, *swaps, *reduces, *bns]:
+    for each in [*swaps, *reduces, *bns]:
         each.wait_send()
 
     def fin_sends(whole):
@@ -856,14 +860,13 @@
     new, field, up, down, kg, out_new, out_field, out_up, out_down, out_kt, out_gn,
     v_new, v_field, v_up, v_down, v_kg, v_kt, v_gn, sem,
 ):
-    held = (v_kg, v_new, v_field, v_up, v_down)
-    reads = [pltpu.make_async_copy(src, dst, sem.at[k]) for k, (src, dst) in enumerate(zip((kg, new, field, up, down), held))]
-    writes = [
-        pltpu.make_async_copy(src, dst, sem.at[5 + k])
-        for k, (src, dst) in enumerate(
-            ((v_new, out_new), (v_field, out_field), (v_up, out_up), (v_down, out_down), (v_kt, out_kt), (v_gn, out_gn))
-        )
-    ]
+    quarters = [(n, slice(4 * k, 4 * k + 4)) for n in range(2) for k in range(4)]
+    ins = [(kg, v_kg)] + [((new, field)[n].at[at], (v_new, v_field)[n].at[at]) for n, at in quarters]
+    outs = [((v_new, v_field)[n].at[at], (out_new, out_field)[n].at[at]) for n, at in quarters]
+    ins += [(up, v_up), (down, v_down)]
+    outs += [(v_up, out_up), (v_down, out_down), (v_kt, out_kt), (v_gn, out_gn)]
+    reads = [pltpu.make_async_copy(src, dst, sem.at[k]) for k, (src, dst) in enumerate(ins)]
+    writes = [pltpu.make_async_copy(src, dst, sem.at[len(ins) + k]) for k, (src, dst) in enumerate(outs)]
     for each in reads:
         each.start()
     reads[0].wait()
@@ -871,9 +874,9 @@
         moved = v_kg[...] if i == 0 else pltpu.roll(v_kg[...], 128 - 32 * i, 1)
         v_kt[i : i + 1, :] = moved[:, 0:9]
         v_gn[0:1, i : i + 1] = moved[:, 9:10]
-    writes[4].start()
-    writes[5].start()
-    for k in range(4):
+    writes[10].start()
+    writes[11].start()
+    for k in range(10):
         reads[1 + k].wait()
         writes[k].start()
     for each in writes:
@@ -945,7 +948,7 @@
         out_specs=(anywhere,) * 6,
         scratch_shapes=[
             buf(16, 16, 256), buf(16, 16, 256), buf(4, 1024), buf(16, 256), buf(1, 128), buf(4, 9), buf(1, 4),
-            pltpu.SemaphoreType.DMA((11,)),
+            pltpu.SemaphoreType.DMA((23,)),
         ],
         compiler_params=pltpu.CompilerParams(vmem_limit_bytes=60 * 1024 * 1024),
         name="results",

time: 65 us -> 63.5 us (0.977)
  Pallas kernels: 63.9 us -> 62.7 us
    pallas_call x1, Pallas kernels: 62 us -> 60.8 us  [shards(): pl.pallas_call(kernel, out_shape=(jax.ShapeDtypeStruct((16, 16, 256), F32...]
where the time goes in v6:
time: 63.5 us; the launch traced here: 63.3 us
  Pallas kernels  62.7 us (99%)
  between operations  0.64 us (1%)
    pallas_call x1, Pallas kernels, shards(): pl.pallas_call(kernel, out_shape=(jax.ShapeDtypeStruct((16, 16, 256), F32...  60.8 us
    pallas_call x1, Pallas kernels, shards(): pl.pallas_call(results, out_shape=(jax.ShapeDtypeStruct((16, 16, 256), F3...  1.9 us

profile of v6, /device:TPU:1, one launch (start us, length us, event | category | flops | bytes accessed | tf_op | source)
XLA Modules:
  0.0 63.3 jit_solution(7720931127198432657)
XLA Ops:
  0.6 60.8 %block.1 = (f32[16,16,256]{2,1,0:T(8,128)}, f32[16,16,256]{2,1,0:T(8,128)}, f32[4,1024]{1,0:T(4,128)}, f32[16,256]{1,0:T(8,128)}, f32[1,128]{1,0:T(1,128)}) custom-call(f32[16,16,256]{2,1,0:T(8,128)} %bitcast.9, f32[16,16,256]{2,1,0:T(8,128)} %bitcast.10, f32[4,1024]{1,0:T(4,128)} %up_in.1, f32[16,256]{1,0:T(8,128)} %down_in.1, f32[4,9]{1,0:T(4,128)} %bitcast.11, ...), custom_call_target="tpu_custom_call" | custom-call | tf_op jit(solution)/shard_map/block/pallas_call | solution.py:895
  61.4 1.9 %results.1 = (f32[16,16,256]{2,1,0:T(8,128)}, f32[16,16,256]{2,1,0:T(8,128)}, f32[4,1024]{1,0:T(4,128)}, f32[16,256]{1,0:T(8,128)}, f32[4,9]{1,0:T(4,128)}, /*index=5*/f32[1,4]{1,0:T(1,128)}) custom-call(f32[16,16,256]{2,1,0:T(8,128)} %get-tuple-element.17.new, f32[16,16,256]{2,1,0:T(8,128)} %get-tuple-element.18.field, f32[4,1024]{1,0:T(4,128)} %get-tuple-element.19.up, ...), custom_call_target="tpu_custom_call" | custom-call | tf_op jit(solution)/shard_map/results/pallas_call | solution.py:937

commit v7 on v6

--- a/solution.py
+++ b/solution.py
@@ -666,22 +666,6 @@
         each.start()
         kgs.append(each)
 
-    def early_sent(whole):
-        for each in own_sends(whole) + ([] if whole else y_sends()):
-            each.wait_send()
-
-        @pl.when(ends == 0)
-        def _():
-            for each in cross_sends(whole) + kg_cross():
-                each.wait_send()
-
-    both(early_sent)
-    for k in range(NY):
-        for each in x_sends(k):
-            each.wait_send()
-    for each in [*small_sends(), *we, *kg1, *ns, *kg2, cot_copy, *norm_copies]:
-        each.wait_send()
-
     for yh in range(2):
         half = pl.ds(4 * yh, 4)
         for dx in (1, 3, 2):
@@ -746,6 +730,22 @@
         each = copy(kgr_x.at[x], kgr_x.at[x], R_KX + k, device(xs_at[k], h, y, l, c))
         each.start()
         kgs.append(each)
+
+    def early_sent(whole):
+        for each in own_sends(whole) + ([] if whole else y_sends()):
+            each.wait_send()
+
+        @pl.when(ends == 0)
+        def _():
+            for each in cross_sends(whole) + kg_cross():
+                each.wait_send()
+
+    both(early_sent)
+    for k in range(NY):
+        for each in x_sends(k):
+            each.wait_send()
+    for each in [*small_sends(), *we, *kg1, *ns, *kg2, cot_copy, *norm_copies]:
+        each.wait_send()
 
     for k in range(1, NY):
         arrived(y_recv.at[k], R_Y + k)

time: 63.5 us -> 63.5 us (level)
  no operation moved by 1% of the time
where the time goes in v7:
time: 63.5 us; the launch traced here: 63.3 us
  Pallas kernels  62.7 us (99%)
  between operations  0.64 us (1%)
    pallas_call x1, Pallas kernels, shards(): pl.pallas_call(kernel, out_shape=(jax.ShapeDtypeStruct((16, 16, 256), F32...  60.8 us
    pallas_call x1, Pallas kernels, shards(): pl.pallas_call(results, out_shape=(jax.ShapeDtypeStruct((16, 16, 256), F3...  1.9 us

profile of v7, /device:TPU:1, one launch (start us, length us, event | category | flops | bytes accessed | tf_op | source)
XLA Modules:
  0.0 63.3 jit_solution(9160610372547652038)
XLA Ops:
  0.6 60.8 %block.1 = (f32[16,16,256]{2,1,0:T(8,128)}, f32[16,16,256]{2,1,0:T(8,128)}, f32[4,1024]{1,0:T(4,128)}, f32[16,256]{1,0:T(8,128)}, f32[1,128]{1,0:T(1,128)}) custom-call(f32[16,16,256]{2,1,0:T(8,128)} %bitcast.9, f32[16,16,256]{2,1,0:T(8,128)} %bitcast.10, f32[4,1024]{1,0:T(4,128)} %up_in.1, f32[16,256]{1,0:T(8,128)} %down_in.1, f32[4,9]{1,0:T(4,128)} %bitcast.11, ...), custom_call_target="tpu_custom_call" | custom-call | tf_op jit(solution)/shard_map/block/pallas_call | solution.py:895
  61.4 1.9 %results.1 = (f32[16,16,256]{2,1,0:T(8,128)}, f32[16,16,256]{2,1,0:T(8,128)}, f32[4,1024]{1,0:T(4,128)}, f32[16,256]{1,0:T(8,128)}, f32[4,9]{1,0:T(4,128)}, /*index=5*/f32[1,4]{1,0:T(1,128)}) custom-call(f32[16,16,256]{2,1,0:T(8,128)} %get-tuple-element.17.new, f32[16,16,256]{2,1,0:T(8,128)} %get-tuple-element.18.field, f32[4,1024]{1,0:T(4,128)} %get-tuple-element.19.up, ...), custom_call_target="tpu_custom_call" | custom-call | tf_op jit(solution)/shard_map/results/pallas_call | solution.py:937
